TPU v7x, 32 devices: a whole 2x2x4 slice. The times are simulated.
32 devices in a mesh: dp: 4 (over z), blk: 2 (over x), uly: 4 (over y, core).
Axes of the slice: x: 2, y: 2, z: 4, core: 2. Of those that a mesh axis runs over, the one named last changes fastest.
Arguments:
- tokens: bfloat16 [8, 1024, 768], P('dp', ('blk', 'uly')), may hold values from -6 to 6
- cotangent: bfloat16 [8, 1024, 768], P('dp', ('blk', 'uly')), may hold values from -6 to 6
- segments: int32 [8, 1024], P('dp', ('blk', 'uly')), may hold values from 0 to 1, as said below
- noised: int32 [8, 1024], P('dp', ('blk', 'uly')), may hold values 0 or 1
- levels: int32 [8], P('dp'), may hold values from 0 to 127
- ada_weight: bfloat16 [2, 4608, 128], P(None, 'dp'), may hold values from -0.5 to 0.5
- ada_bias: bfloat16 [2, 4608], P(None, 'dp'), may hold values from -1.75 to 1.75
- first_gain: bfloat16 [2, 768], P(None, 'dp'), may hold values from 0.5 to 1.5
- qkv_weight: bfloat16 [2, 768, 2304], P(None, 'dp'), may hold values from -0.21875 to 0.21875
- out_weight: bfloat16 [2, 768, 768], P(None, 'dp'), may hold values from -4 to 4
- second_gain: bfloat16 [2, 768], P(None, 'dp'), may hold values from 0.5 to 1.5
- hidden_weight: bfloat16 [2, 768, 3072], P(None, 'dp'), may hold values from -0.21875 to 0.21875
- hidden_bias: bfloat16 [2, 3072], P(None, 'dp'), may hold values from -1.75 to 1.75
- down_weight: bfloat16 [2, 3072, 768], P(None, 'dp'), may hold values from -0.109375 to 0.109375
- down_bias: bfloat16 [2, 768], P(None, 'dp'), may hold values from -1.75 to 1.75
Outputs:
- output: bfloat16 [8, 1024, 768], P('dp', ('blk', 'uly'))
- tokens_grad: bfloat16 [8, 1024, 768], P('dp', ('blk', 'uly'))
- ada_weight_grad: float32 [2, 4608, 128], P(None, 'dp')
- ada_bias_grad: float32 [2, 4608], P(None, 'dp')
- first_gain_grad: float32 [2, 768], P(None, 'dp')
- qkv_weight_grad: float32 [2, 768, 2304], P(None, 'dp')
- out_weight_grad: float32 [2, 768, 768], P(None, 'dp')
- second_gain_grad: float32 [2, 768], P(None, 'dp')
- hidden_weight_grad: float32 [2, 768, 3072], P(None, 'dp')
- hidden_bias_grad: float32 [2, 3072], P(None, 'dp')
- down_weight_grad: float32 [2, 3072, 768], P(None, 'dp')
- down_bias_grad: float32 [2, 768], P(None, 'dp')
Inputs may be any that keep to these rules, and one draw needn't show every extreme that they name: `segments`: in each group of 2 consecutive rows exactly one row, drawn from the seed, is a single document (ids all 0); every other row is packed: its id at position t is (t + off) // 1024 for an offset off of 1 to 1023 drawn for the row.
All inputs are finite; a program needn't handle non-finite values. No bound on the sum of `noised` on one device may be relied on, other than what follows from the above.
Results may differ from a plain program's by a relative error of at most 0.019.
Values may be sent and summed in bfloat16 or wider, within the bound.
No kernel may reach another device: no remote copies, remote signals or barrier semaphores. Data moves between devices by JAX's collectives and lax.ppermute only.
A program may use at most 256 MiB of HBM per device.

v0:
```python
import math

import jax
import jax.numpy as jnp
from jax import lax
from jax.experimental import pallas as pl
from jax.experimental.pallas import tpu as pltpu
from jax.sharding import PartitionSpec as P

HEADS = 12


epsilon = 1e-05
neg_big = -1e30


def cond_vector(levels, width):
    half_width = width // 2
    freqs = jnp.exp(-math.log(10000.0) * jnp.arange(half_width, dtype=jnp.float32) / half_width)
    angles = levels.astype(jnp.float32)[:, None] * freqs[None, :]
    return jax.nn.silu(jnp.concatenate([jnp.cos(angles), jnp.sin(angles)], axis=-1))


def norm_mod(values, gain_vec, shift_vec, scale_vec):
    average = jnp.mean(values, axis=-1, keepdims=True)
    centered = values - average
    variance = jnp.mean(centered * centered, axis=-1, keepdims=True)
    return centered * lax.rsqrt(variance + epsilon) * gain_vec * (1.0 + scale_vec) + shift_vec


def gelu_tanh(values):
    return jax.nn.gelu(values, approximate=True)


def left_product(first, second):
    return lax.dot_general(
        first, second, (((0,), (0,)), ((), ())), preferred_element_type=jnp.float32
    )


def right_product(first, second):
    return lax.dot_general(
        first, second, (((1,), (1,)), ((), ())), preferred_element_type=jnp.float32
    )


def fetch(params, layer_index):
    p_ada, p_bias, p_gain, p_qkv, p_out, p_gain_two, p_hidden, p_hbias, p_down, p_dbias = params
    return (
        lax.all_gather(p_ada[layer_index], "dp", axis=0, tiled=True),
        lax.all_gather(p_bias[layer_index], "dp", axis=0, tiled=True),
        lax.all_gather(p_gain[layer_index], "dp", axis=0, tiled=True),
        lax.all_gather(p_qkv[layer_index], "dp", axis=0, tiled=True),
        lax.all_gather(p_out[layer_index], "dp", axis=0, tiled=True),
        lax.all_gather(p_gain_two[layer_index], "dp", axis=0, tiled=True),
        lax.all_gather(p_hidden[layer_index], "dp", axis=0, tiled=True),
        lax.all_gather(p_hbias[layer_index], "dp", axis=0, tiled=True),
        lax.all_gather(p_down[layer_index], "dp", axis=0, tiled=True),
        lax.all_gather(p_dbias[layer_index], "dp", axis=0, tiled=True),
    )


def reduce_grads(grads):
    shards = (
        lax.psum_scatter(
            grads[0].astype(jnp.bfloat16), "dp", scatter_dimension=0, tiled=True
        ).astype(jnp.float32),
        lax.psum_scatter(
            grads[1].astype(jnp.bfloat16), "dp", scatter_dimension=0, tiled=True
        ).astype(jnp.float32),
        lax.psum_scatter(
            grads[2].astype(jnp.bfloat16), "dp", scatter_dimension=0, tiled=True
        ).astype(jnp.float32),
        lax.psum_scatter(
            grads[3].astype(jnp.bfloat16), "dp", scatter_dimension=0, tiled=True
        ).astype(jnp.float32),
        lax.psum_scatter(
            grads[4].astype(jnp.bfloat16), "dp", scatter_dimension=0, tiled=True
        ).astype(jnp.float32),
        lax.psum_scatter(
            grads[5].astype(jnp.bfloat16), "dp", scatter_dimension=0, tiled=True
        ).astype(jnp.float32),
        lax.psum_scatter(
            grads[6].astype(jnp.bfloat16), "dp", scatter_dimension=0, tiled=True
        ).astype(jnp.float32),
        lax.psum_scatter(
            grads[7].astype(jnp.bfloat16), "dp", scatter_dimension=0, tiled=True
        ).astype(jnp.float32),
        lax.psum_scatter(
            grads[8].astype(jnp.bfloat16), "dp", scatter_dimension=0, tiled=True
        ).astype(jnp.float32),
        lax.psum_scatter(
            grads[9].astype(jnp.bfloat16), "dp", scatter_dimension=0, tiled=True
        ).astype(jnp.float32),
    )
    return (
        lax.psum(shards[0].astype(jnp.bfloat16), ("blk", "uly")).astype(jnp.float32),
        lax.psum(shards[1].astype(jnp.bfloat16), ("blk", "uly")).astype(jnp.float32),
        lax.psum(shards[2].astype(jnp.bfloat16), ("blk", "uly")).astype(jnp.float32),
        lax.psum(shards[3].astype(jnp.bfloat16), ("blk", "uly")).astype(jnp.float32),
        lax.psum(shards[4].astype(jnp.bfloat16), ("blk", "uly")).astype(jnp.float32),
        lax.psum(shards[5].astype(jnp.bfloat16), ("blk", "uly")).astype(jnp.float32),
        lax.psum(shards[6].astype(jnp.bfloat16), ("blk", "uly")).astype(jnp.float32),
        lax.psum(shards[7].astype(jnp.bfloat16), ("blk", "uly")).astype(jnp.float32),
        lax.psum(shards[8].astype(jnp.bfloat16), ("blk", "uly")).astype(jnp.float32),
        lax.psum(shards[9].astype(jnp.bfloat16), ("blk", "uly")).astype(jnp.float32),
    )


def over_blocks(block_fn, carry, key_piece, value_piece, seg_piece):
    count = key_piece.shape[2]
    size = 512

    def block_step(inner, position):
        offset = position * size
        key_blk = lax.dynamic_slice_in_dim(key_piece, offset, size, 2)
        value_blk = lax.dynamic_slice_in_dim(value_piece, offset, size, 2)
        seg_blk = lax.dynamic_slice_in_dim(seg_piece, offset, size, 0)
        return (block_fn(inner, key_blk, value_blk, seg_blk, offset), None)

    return lax.scan(block_step, carry, jnp.arange(count // size, dtype=jnp.int32))[0]


def split_heads(qkv_b):
    tokens_dev = qkv_b.shape[0]
    width = qkv_b.shape[1] // 3
    heads_all = lax.all_to_all(
        qkv_b.reshape(tokens_dev, 3, width), "uly", split_axis=2, concat_axis=0, tiled=True
    )
    span = heads_all.shape[0]
    head_dim = width // HEADS
    local_heads = heads_all.shape[2] // head_dim
    layout = heads_all.reshape(span, 3, local_heads, head_dim).transpose(1, 2, 3, 0)
    return (layout[0], layout[1], layout[2])


def layer_forward(state, weights_now, cond_b, seg_row):
    (
        ada_weight,
        ada_bias,
        first_gain,
        qkv_weight,
        out_weight,
        second_gain,
        hidden_weight,
        hidden_bias,
        down_weight,
        down_bias,
    ) = weights_now
    modulation = jnp.dot(ada_weight, cond_b, preferred_element_type=jnp.float32) + ada_bias.astype(
        jnp.float32
    )
    shift_one, scale_one, gate_one, shift_two, scale_two, gate_two = jnp.split(modulation, 6)
    normed_b = norm_mod(state, first_gain.astype(jnp.float32), shift_one, scale_one).astype(
        jnp.bfloat16
    )
    qkv_b = jnp.dot(normed_b, qkv_weight, preferred_element_type=jnp.float32).astype(jnp.bfloat16)
    query_t, key_t, value_t = split_heads(qkv_b)
    local_heads, head_dim, span = query_t.shape
    factor = head_dim ** (-0.5)
    query_seg = lax.dynamic_slice_in_dim(seg_row, lax.axis_index("blk") * span, span, 0)

    def forward_block(carry, key_blk, value_blk, seg_blk, start):
        running_max, running_total, weighted = carry
        scores = (
            jnp.einsum("hdq,hdk->hqk", query_t, key_blk, preferred_element_type=jnp.float32)
            * factor
        )
        allowed = (query_seg[:, None] == seg_blk[None, :])[None]
        masked = jnp.where(allowed, scores, neg_big)
        new_max = jnp.maximum(running_max, jnp.max(masked, axis=-1))
        probabilities = jnp.where(allowed, jnp.exp(masked - new_max[..., None]), 0.0)
        rescale = jnp.exp(running_max - new_max)
        running_total = running_total * rescale + jnp.sum(probabilities, axis=-1)
        update = jnp.einsum(
            "hqk,hdk->hdq",
            probabilities.astype(jnp.bfloat16),
            value_blk,
            preferred_element_type=jnp.float32,
        )
        weighted = weighted * rescale[:, None, :] + update
        return (new_max, running_total, weighted)

    initial = (
        jnp.full((local_heads, span), neg_big, jnp.float32),
        jnp.zeros((local_heads, span), jnp.float32),
        jnp.zeros((local_heads, head_dim, span), jnp.float32),
    )
    running_max, running_total, weighted = over_blocks(
        forward_block,
        initial,
        lax.all_gather(key_t, "blk", axis=2, tiled=True),
        lax.all_gather(value_t, "blk", axis=2, tiled=True),
        seg_row,
    )
    attended_heads = weighted / running_total[:, None, :]
    log_total = running_max + jnp.log(running_total)
    sendable = (
        attended_heads.astype(jnp.bfloat16).transpose(2, 0, 1).reshape(span, local_heads * head_dim)
    )
    attended_b = lax.all_to_all(sendable, "uly", split_axis=0, concat_axis=1, tiled=True)
    branch_one = jnp.dot(attended_b, out_weight, preferred_element_type=jnp.float32)
    middle = state + gate_one * branch_one
    normed_two = norm_mod(middle, second_gain.astype(jnp.float32), shift_two, scale_two).astype(
        jnp.bfloat16
    )
    hidden_pre = jnp.dot(
        normed_two, hidden_weight, preferred_element_type=jnp.float32
    ) + hidden_bias.astype(jnp.float32)
    activated = gelu_tanh(hidden_pre).astype(jnp.bfloat16)
    branch_two = jnp.dot(
        activated, down_weight, preferred_element_type=jnp.float32
    ) + down_bias.astype(jnp.float32)
    result = middle + gate_two * branch_two
    kept = (
        state,
        modulation,
        normed_b,
        query_t,
        key_t,
        value_t,
        attended_heads,
        log_total,
        attended_b,
        branch_one,
        middle,
        normed_two,
        hidden_pre,
        activated,
        branch_two,
    )
    return (result, kept)


def layer_backward(grad, weights_now, kept, cond_b, seg_row):
    (
        ada_weight,
        ada_bias,
        first_gain,
        qkv_weight,
        out_weight,
        second_gain,
        hidden_weight,
        hidden_bias,
        down_weight,
        down_bias,
    ) = weights_now
    (
        state,
        modulation,
        normed_b,
        query_t,
        key_t,
        value_t,
        attended_heads,
        log_total,
        attended_b,
        branch_one,
        middle,
        normed_two,
        hidden_pre,
        activated,
        branch_two,
    ) = kept
    shift_one, scale_one, gate_one, shift_two, scale_two, gate_two = jnp.split(modulation, 6)
    gain_one = first_gain.astype(jnp.float32)
    gain_two = second_gain.astype(jnp.float32)
    d_gate_two = jnp.sum(grad * branch_two, axis=0)
    d_branch_two = (gate_two * grad).astype(jnp.bfloat16)
    d_down_weight = left_product(activated, d_branch_two)
    d_down_bias = jnp.sum(d_branch_two.astype(jnp.float32), axis=0)
    d_activated = right_product(d_branch_two, down_weight)
    gelu_back = jax.vjp(gelu_tanh, hidden_pre)[1]
    d_pre = gelu_back(d_activated)[0].astype(jnp.bfloat16)
    d_hidden_weight = left_product(normed_two, d_pre)
    d_hidden_bias = jnp.sum(d_pre.astype(jnp.float32), axis=0)
    d_normed_two = right_product(d_pre, hidden_weight)
    norm_back_two = jax.vjp(norm_mod, middle, gain_two, shift_two, scale_two)[1]
    d_middle_part, d_gain_two, d_shift_two, d_scale_two = norm_back_two(d_normed_two)
    d_middle = grad + d_middle_part
    d_gate_one = jnp.sum(d_middle * branch_one, axis=0)
    d_branch_one = (gate_one * d_middle).astype(jnp.bfloat16)
    d_out_weight = left_product(attended_b, d_branch_one)
    d_attended_b = right_product(d_branch_one, out_weight).astype(jnp.bfloat16)
    local_heads, head_dim, span = query_t.shape
    factor = head_dim ** (-0.5)
    d_heads_t = (
        lax.all_to_all(d_attended_b, "uly", split_axis=1, concat_axis=0, tiled=True)
        .reshape(span, local_heads, head_dim)
        .transpose(1, 2, 0)
    )
    row_delta = jnp.sum(d_heads_t.astype(jnp.float32) * attended_heads, axis=1)
    query_seg = lax.dynamic_slice_in_dim(seg_row, lax.axis_index("blk") * span, span, 0)

    def backward_block(carry, key_blk, value_blk, seg_blk, start):
        d_query, d_key_all, d_value_all = carry
        scores = (
            jnp.einsum("hdq,hdk->hqk", query_t, key_blk, preferred_element_type=jnp.float32)
            * factor
        )
        allowed = (query_seg[:, None] == seg_blk[None, :])[None]
        probabilities = jnp.where(allowed, jnp.exp(scores - log_total[..., None]), 0.0)
        d_probs = jnp.einsum(
            "hdq,hdk->hqk", d_heads_t, value_blk, preferred_element_type=jnp.float32
        )
        d_scores = (probabilities * (d_probs - row_delta[..., None])).astype(jnp.bfloat16)
        d_query = (
            d_query
            + jnp.einsum("hqk,hdk->hdq", d_scores, key_blk, preferred_element_type=jnp.float32)
            * factor
        )
        d_key_new = (
            jnp.einsum("hqk,hdq->hdk", d_scores, query_t, preferred_element_type=jnp.float32)
            * factor
        )
        d_value_new = jnp.einsum(
            "hqk,hdq->hdk",
            probabilities.astype(jnp.bfloat16),
            d_heads_t,
            preferred_element_type=jnp.float32,
        )
        size = key_blk.shape[2]
        d_key_all = lax.dynamic_update_slice_in_dim(
            d_key_all, lax.dynamic_slice_in_dim(d_key_all, start, size, 2) + d_key_new, start, 2
        )
        d_value_all = lax.dynamic_update_slice_in_dim(
            d_value_all,
            lax.dynamic_slice_in_dim(d_value_all, start, size, 2) + d_value_new,
            start,
            2,
        )
        return (d_query, d_key_all, d_value_all)

    row_len = seg_row.shape[0]
    initial = (
        jnp.zeros((local_heads, head_dim, span), jnp.float32),
        jnp.zeros((local_heads, head_dim, row_len), jnp.float32),
        jnp.zeros((local_heads, head_dim, row_len), jnp.float32),
    )
    d_query, d_key_all, d_value_all = over_blocks(
        backward_block,
        initial,
        lax.all_gather(key_t, "blk", axis=2, tiled=True),
        lax.all_gather(value_t, "blk", axis=2, tiled=True),
        seg_row,
    )
    d_key, d_value = (
        lax.psum_scatter(
            d_key_all.astype(jnp.bfloat16), "blk", scatter_dimension=2, tiled=True
        ).astype(jnp.float32),
        lax.psum_scatter(
            d_value_all.astype(jnp.bfloat16), "blk", scatter_dimension=2, tiled=True
        ).astype(jnp.float32),
    )
    joined = jnp.stack([d_query, d_key, d_value], axis=0).astype(jnp.bfloat16)
    stacked = joined.transpose(3, 0, 1, 2).reshape(span, 3, local_heads * head_dim)
    returned = lax.all_to_all(stacked, "uly", split_axis=0, concat_axis=2, tiled=True)
    tokens_dev = state.shape[0]
    d_qkv_b = returned.reshape(tokens_dev, returned.shape[1] * returned.shape[2])
    d_qkv_weight = left_product(normed_b, d_qkv_b)
    d_normed = right_product(d_qkv_b, qkv_weight)
    norm_back_one = jax.vjp(norm_mod, state, gain_one, shift_one, scale_one)[1]
    d_state_part, d_gain_one, d_shift_one, d_scale_one = norm_back_one(d_normed)
    d_state = d_middle + d_state_part
    d_modulation = jnp.concatenate(
        [d_shift_one, d_scale_one, d_gate_one, d_shift_two, d_scale_two, d_gate_two]
    )
    d_ada_weight = d_modulation[:, None] * cond_b.astype(jnp.float32)[None, :]
    grads = (
        d_ada_weight,
        d_modulation,
        d_gain_one,
        d_qkv_weight,
        d_out_weight,
        d_gain_two,
        d_hidden_weight,
        d_hidden_bias,
        d_down_weight,
        d_down_bias,
    )
    return (d_state, grads)


def add_tuples(first, second):
    if first is None:
        return second
    return tuple((left_item + right_item for left_item, right_item in zip(first, second)))


def local(
    tokens,
    cotangent,
    segments,
    noised,
    levels,
    ada_weight,
    ada_bias,
    first_gain,
    qkv_weight,
    out_weight,
    second_gain,
    hidden_weight,
    hidden_bias,
    down_weight,
    down_bias,
):
    params = (
        ada_weight,
        ada_bias,
        first_gain,
        qkv_weight,
        out_weight,
        second_gain,
        hidden_weight,
        hidden_bias,
        down_weight,
        down_bias,
    )
    layers = ada_weight.shape[0]
    batches = tokens.shape[0]
    row_segs = lax.all_gather(segments, ("blk", "uly"), axis=1, tiled=True)
    conds = cond_vector(levels, ada_weight.shape[2]).astype(jnp.bfloat16)
    stored = [fetch(params, layer_index) for layer_index in range(layers)]
    sums = [None] * layers
    outputs = []
    input_grads = []
    for batch_index in range(batches):
        state = tokens[batch_index].astype(jnp.float32)
        cond_b = conds[batch_index]
        seg_row = row_segs[batch_index]
        kept_all = []
        for layer_index in range(layers):
            weights_now = stored[layer_index]
            state, kept = layer_forward(state, weights_now, cond_b, seg_row)
            kept_all.append(kept)
        outputs.append(state.astype(jnp.bfloat16))
        grad = (
            cotangent[batch_index].astype(jnp.float32)
            * noised[batch_index].astype(jnp.float32)[:, None]
        )
        for layer_index in reversed(range(layers)):
            weights_now = stored[layer_index]
            grad, grads = layer_backward(grad, weights_now, kept_all[layer_index], cond_b, seg_row)
            sums[layer_index] = add_tuples(sums[layer_index], reduce_grads(grads))
        input_grads.append(grad.astype(jnp.bfloat16))
    stacked = [
        jnp.stack([sums[layer_index][member] for layer_index in range(layers)])
        for member in range(10)
    ]
    return (
        jnp.stack(outputs),
        jnp.stack(input_grads),
        stacked[0],
        stacked[1],
        stacked[2],
        stacked[3],
        stacked[4],
        stacked[5],
        stacked[6],
        stacked[7],
        stacked[8],
        stacked[9],
    )


SWAP = [(0, 1), (1, 0)]
PAIR = [(0, 1), (1, 0), (2, 3), (3, 2)]
ACROSS = [(0, 2), (2, 0), (1, 3), (3, 1)]
VMEM_BYTES = 16 * 1024 * 1024
COPY_BYTES = 12 * 1024 * 1024
FREE = pl.CostEstimate(flops=0, bytes_accessed=0, transcendentals=0)
COPIES = pl.CostEstimate(flops=0, bytes_accessed=7_000_000, transcendentals=0)


def swap_blk(value):
    return lax.ppermute(value, "blk", SWAP)


def swap_half(value):
    return lax.ppermute(value, "uly", PAIR)


def swap_core(value):
    return lax.ppermute(value, "uly", ACROSS)


def from_shard(value, back, shards):
    return lax.ppermute(value, "dp", [(at, (at + back) % shards) for at in range(shards)])


def plain_product(first, second):
    return jnp.dot(first, second, preferred_element_type=jnp.float32)


def normalise(values):
    average = jnp.mean(values, axis=-1, keepdims=True)
    centered = values - average
    variance = jnp.mean(centered * centered, axis=-1, keepdims=True)
    inverse = lax.rsqrt(variance + epsilon)
    return centered * inverse, inverse


def pick(array, index, axis):
    return lax.dynamic_index_in_dim(array, index, axis, keepdims=False)


def low(value):
    return value.astype(jnp.bfloat16)


def wide(value):
    return value.astype(jnp.float32)


def token(array):
    while array.ndim > 2:
        array = array[0]
    return array[:16, :128]


def whole_call(kernel, name, shapes, operands, place=None, after=()):
    specs = [] if place is None else [pl.BlockSpec(memory_space=pltpu.SMEM)]
    specs += [pl.BlockSpec(memory_space=pltpu.VMEM)] * len(operands)
    specs += [pl.BlockSpec(memory_space=pl.ANY)] * len(after)
    count = len(operands) + (place is not None)

    def body(*refs):
        kernel(*refs[:count], *refs[count + len(after) :])

    return pl.pallas_call(
        body,
        out_shape=tuple(jax.ShapeDtypeStruct(shape, kind) for shape, kind in shapes),
        in_specs=specs,
        out_specs=(pl.BlockSpec(memory_space=pltpu.VMEM),) * len(shapes),
        compiler_params=pltpu.CompilerParams(vmem_limit_bytes=VMEM_BYTES),
        cost_estimate=FREE,
        name=name,
    )(*([] if place is None else [place]), *operands, *after)


def hold(value, *after):
    return pl.pallas_call(
        lambda *refs: None,
        out_shape=jax.ShapeDtypeStruct(value.shape, value.dtype),
        in_specs=[pl.BlockSpec(memory_space=pl.ANY)] * (1 + len(after)),
        out_specs=pl.BlockSpec(memory_space=pl.ANY),
        input_output_aliases={0: 0},
        cost_estimate=FREE,
        name="hold",
    )(value, *after)


def run_copies(pairs, sems):
    copies = [
        pltpu.make_async_copy(source, target, sems.at[number])
        for number, (source, target) in enumerate(pairs)
    ]
    for copy in copies:
        copy.start()
    for copy in copies:
        copy.wait()


def attn_pairs(sizes, layer, rows, core, qkv_ref, target_ref):
    rows_in, rows_down, half, hidden_cut, shards = sizes
    lanes = pl.multiple_of(core * half, 128)
    pairs = [
        (
            qkv_ref.at[layer, rows, pl.ds(kind * 2 * half + lanes, half)],
            target_ref.at[:, pl.ds(kind * half, half)],
        )
        for kind in range(3)
    ]
    return pairs


def hidden_pairs(sizes, layer, rows, core, hidden_ref, target_ref):
    rows_in, rows_down, half, hidden_cut, shards = sizes
    lanes = pl.multiple_of(core * hidden_cut, 128)
    return [
        (
            hidden_ref.at[layer, rows, pl.ds(at * 2 * hidden_cut + lanes, hidden_cut)],
            target_ref.at[:, pl.ds(at * hidden_cut, hidden_cut)],
        )
        for at in range(shards)
    ]


def down_pairs(sizes, layer, place_ref, down_ref, target_ref):
    rows_in, rows_down, half, hidden_cut, shards = sizes
    first = pl.multiple_of(place_ref[2] * hidden_cut + place_ref[1] * rows_down, 16)
    return [
        (
            down_ref.at[layer, pl.ds(first + side * rows_in, rows_in)],
            target_ref.at[:, pl.ds(side * 2 * half, 2 * half)],
        )
        for side in range(2)
    ]


def mlp_pairs(sizes, layer, place_ref, out_ref, hidden_ref, down_ref, target_ref):
    rows_in, rows_down, half, hidden_cut, shards = sizes
    rows = pl.ds(pl.multiple_of(place_ref[1] * rows_in, 16), rows_in)
    above, below = target_ref.at[pl.ds(0, rows_in)], target_ref.at[pl.ds(rows_in, rows_in)]
    pairs = hidden_pairs(sizes, layer, rows, place_ref[2], hidden_ref, above)
    pairs += down_pairs(sizes, layer, place_ref, down_ref, below)
    for number, part_ref in enumerate((above, below)):
        pairs.append(
            (out_ref.at[layer, rows, pl.ds(number * half, half)], part_ref.at[:, pl.ds(4 * half, half)])
        )
    return pairs


def cut_attn_kernel(sizes, layer, place_ref, qkv_ref, *refs):
    piece_ref, sems = refs[-2:]
    rows = pl.ds(pl.multiple_of(place_ref[1] * sizes[0], 16), sizes[0])
    run_copies(attn_pairs(sizes, layer, rows, place_ref[2], qkv_ref, piece_ref), sems)


def cut_mlp_kernel(sizes, layer, place_ref, out_ref, hidden_ref, down_ref, *refs):
    piece_ref, sems = refs[-2:]
    run_copies(mlp_pairs(sizes, layer, place_ref, out_ref, hidden_ref, down_ref, piece_ref), sems)


def cut_next_kernel(sizes, layer, place_ref, qkv_ref, out_ref, hidden_ref, down_ref, *refs):
    piece_ref, sems = refs[-2:]
    rows_in, rows_down, half, hidden_cut, shards = sizes
    rows = pl.ds(pl.multiple_of(place_ref[1] * rows_in, 16), rows_in)
    pairs = mlp_pairs(
        sizes, layer, place_ref, out_ref, hidden_ref, down_ref, piece_ref.at[pl.ds(0, 2 * rows_in)]
    )
    pairs += attn_pairs(
        sizes, layer, rows, place_ref[2], qkv_ref,
        piece_ref.at[pl.ds(2 * rows_in, rows_in), pl.ds(0, 3 * half)],
    )
    piece_ref[2 * rows_in :, 3 * half :] = jnp.zeros((rows_in, 2 * half), piece_ref.dtype)
    run_copies(pairs, sems)


def others_kernel(cuts, place_ref, all_ref, *refs):
    outs, sems = refs[-1 - len(cuts) : -1], refs[-1]
    shards = all_ref.shape[0]
    pairs = []
    for (first, rows, columns), out_ref in zip(cuts, outs):
        for back in range(1, shards):
            source = all_ref.at[
                lax.rem(place_ref[0] + shards - back, shards), pl.ds(first, rows), pl.ds(0, columns)
            ]
            pairs.append((source, out_ref.at[back - 1]))
    run_copies(pairs, sems)


def others(place, whole, cuts, after=()):
    shards = whole.shape[0]
    return copy_call(
        lambda *refs: others_kernel(cuts, *refs), "others", place, [whole],
        [(shards - 1, rows, columns) for _, rows, columns in cuts], len(cuts) * (shards - 1), after,
    )


def copy_call(kernel, name, place, operands, shapes, count, after=(), keep=False):
    kind = operands[0].dtype
    return pl.pallas_call(
        kernel,
        out_shape=tuple(
            pltpu.VMEM(shape, kind) if keep else jax.ShapeDtypeStruct(shape, kind) for shape in shapes
        ),
        in_specs=[pl.BlockSpec(memory_space=pltpu.SMEM)]
        + [pl.BlockSpec(memory_space=pl.ANY)] * len(operands)
        + [pl.BlockSpec(memory_space=pl.ANY)] * len(after),
        out_specs=(pl.BlockSpec(memory_space=pltpu.VMEM),) * len(shapes),
        scratch_shapes=[pltpu.SemaphoreType.DMA((count,))],
        compiler_params=pltpu.CompilerParams(vmem_limit_bytes=COPY_BYTES),
        cost_estimate=COPIES,
        name=name,
    )(place, *operands, *after)


def join_attn_kernel(sizes, layer, place_ref, qkv_ref, *refs):
    pieces, whole_ref, sems = refs[:4], refs[-2], refs[-1]
    rows_in, shards = sizes[0], sizes[-1]
    shard, quarter = place_ref[0], place_ref[1]
    pairs = attn_pairs(sizes, layer, slice(None), place_ref[2], qkv_ref, whole_ref.at[shard])
    for relative, piece_ref in enumerate(pieces):
        rows = pl.ds(pl.multiple_of((quarter ^ relative) * rows_in, 16), rows_in)
        for back in range(1, shards):
            target = whole_ref.at[lax.rem(shard + shards - back, shards), rows]
            pairs.append((piece_ref.at[back - 1], target))
    run_copies(pairs, sems)


def join_mlp_kernel(sizes, layer, place_ref, out_ref, hidden_ref, down_ref, *refs):
    pieces = refs[:4]
    whole_o_ref, whole_h_ref, whole_d_ref, sems = refs[-4:]
    rows_in, rows_down, half, hidden_cut, shards = sizes
    shard, quarter, core = place_ref[0], place_ref[1], place_ref[2]
    pairs = hidden_pairs(sizes, layer, slice(None), core, hidden_ref, whole_h_ref.at[shard])
    first = pl.multiple_of(core * hidden_cut, 128)
    pairs.append((down_ref.at[layer, pl.ds(first, hidden_cut)], whole_d_ref.at[shard]))
    pairs.append((out_ref.at[layer], whole_o_ref.at[shard]))
    for relative in range(4):
        at_h = pl.multiple_of((quarter ^ relative) * rows_in, 16)
        at_d = pl.multiple_of((quarter ^ relative) * rows_down, 16)
        for back in range(1, shards):
            place = lax.rem(shard + shards - back, shards)
            above = pieces[relative].at[back - 1, pl.ds(0, rows_in)]
            below = pieces[relative].at[back - 1, pl.ds(rows_in, rows_in)]
            pairs.append(
                (above.at[:, pl.ds(0, 4 * half)], whole_h_ref.at[place, pl.ds(at_h, rows_in)])
            )
            for number, part in enumerate((above, below)):
                pairs.append(
                    (
                        below.at[:, pl.ds(number * 2 * half, 2 * half)],
                        whole_d_ref.at[place, pl.ds(at_d + number * rows_in, rows_in)],
                    )
                )
                pairs.append(
                    (
                        part.at[:, pl.ds(4 * half, half)],
                        whole_o_ref.at[place, pl.ds(at_h, rows_in), pl.ds(number * half, half)],
                    )
                )
    run_copies(pairs, sems)


def finish_attn_part(owner, half, rows, piece, qkv_ref, out_ref):
    width = 2 * half
    lanes = pl.multiple_of(owner * half, 128)
    for kind in range(3):
        qkv_ref[0, :, pl.ds(kind * width + lanes, half)] = wide(
            piece[0, :rows, kind * half : (kind + 1) * half]
        )
    out_ref[0, :, pl.ds(lanes, half)] = wide(piece[0, :rows, 3 * half :])


def finish_mlp_part(owner, half, rows, shards, start, piece, hidden_ref, down_ref):
    width = 2 * half
    hidden_cut = hidden_ref.shape[2] // (2 * shards)
    lanes = pl.multiple_of(owner * hidden_cut, 128)
    for at in range(shards):
        hidden_ref[0, :, pl.ds(at * 2 * hidden_cut + lanes, hidden_cut)] = wide(
            piece[0, start : start + rows, at * hidden_cut : (at + 1) * hidden_cut]
        )
    for side in range(2):
        down_ref[0, owner, 0, side * rows : (side + 1) * rows] = wide(
            piece[0, start + rows :, side * width : (side + 1) * width]
        )


def finish_kernel(parts, half, rows, shards, place_ref, *refs):
    outs = refs[len(refs) - 2 * len(parts) :]
    for relative in range(2):
        owner, at = place_ref[2] ^ relative, 0
        for number, part in enumerate(parts):
            if part == "attn":
                finish_attn_part(owner, half, rows, refs[relative], *outs[2 * number : 2 * number + 2])
                at += rows
            else:
                finish_mlp_part(
                    owner, half, rows, shards, at, refs[relative], *outs[2 * number : 2 * number + 2]
                )


def finish(place, layer, parts, pieces, shapes, half, rows, shards, before=None):
    width = 2 * half
    blocks = {
        "attn": [
            pl.BlockSpec((1, rows, 3 * width), lambda at, place: (layer, place[1] ^ at, 0)),
            pl.BlockSpec((1, rows, width), lambda at, place: (layer, place[1] ^ at, 0)),
        ],
        "mlp": [
            pl.BlockSpec((1, rows, shapes["mlp"][0][2]), lambda at, place: (layer, place[1] ^ at, 0)),
            pl.BlockSpec(
                (1, 2, 1, 2 * rows, width), lambda at, place: (layer, 0, place[1] ^ at, 0, 0)
            ),
        ],
    }
    operands, aliases = list(pieces), {}
    specs = [pl.BlockSpec((1, *piece.shape[1:]), lambda at, place: (at, 0, 0)) for piece in pieces]
    if before is not None:
        operands += list(before)
        specs += [pl.BlockSpec(memory_space=pl.ANY)] * len(before)
        aliases = {3 + number: number for number in range(len(before))}
    return pl.pallas_call(
        lambda *refs: finish_kernel(parts, half, rows, shards, *refs),
        grid_spec=pltpu.PrefetchScalarGridSpec(
            num_scalar_prefetch=1,
            grid=(4,),
            in_specs=specs,
            out_specs=tuple(block for part in parts for block in blocks[part]),
        ),
        out_shape=tuple(
            jax.ShapeDtypeStruct(shape, jnp.float32) for part in parts for shape in shapes[part]
        ),
        input_output_aliases=aliases,
        compiler_params=pltpu.CompilerParams(vmem_limit_bytes=VMEM_BYTES),
        cost_estimate=COPIES,
        name="finish",
    )(place, *operands)


TILE = 256
SHIFT_ONE, SCALE_ONE, GATE_ONE, SHIFT_TWO, SCALE_TWO, GATE_TWO, GAIN_ONE, GAIN_TWO, BIAS_DOWN = range(9)


def row_of(ref, number):
    return ref[number : number + 1, :]


def norm_rows(values, vec_ref, gain, scale, shift):
    unit_values, _ = normalise(values)
    return low(
        unit_values * row_of(vec_ref, gain) * (1.0 + row_of(vec_ref, scale)) + row_of(vec_ref, shift)
    )


def enter_kernel(x_ref, vec_ref, n_ref):
    n_ref[...] = norm_rows(wide(x_ref[...]), vec_ref, GAIN_ONE, SCALE_ONE, SHIFT_ONE)


def project_kernel(first, last, own_ref, other_ref, weight_ref, out_ref, *refs):
    count = own_ref.shape[0]
    for chip_ref in refs:
        chip_ref[:count, :] = own_ref[...]
        chip_ref[count:, :] = other_ref[...]
    out_ref[:count, :] = low(plain_product(own_ref[...], weight_ref[:, first:last]))
    out_ref[count:, :] = low(plain_product(other_ref[...], weight_ref[:, first:last]))


def middle_kernel(
    place_ref, att_own_ref, att_other_ref, weight_ref, state_ref, vec_ref, branch_ref, middle_ref, n_ref, att_ref
):
    half = att_own_ref.shape[1]
    att_ref[:, pl.ds(pl.multiple_of(place_ref[2] * half, 128), half)] = att_own_ref[...]
    att_ref[:, pl.ds(pl.multiple_of((1 - place_ref[2]) * half, 128), half)] = att_other_ref[...]
    branch = plain_product(att_ref[...], weight_ref[...])
    middle = state_ref[...] + row_of(vec_ref, GATE_ONE) * branch
    branch_ref[...] = low(branch)
    middle_ref[...] = middle
    n_ref[...] = norm_rows(middle, vec_ref, GAIN_TWO, SCALE_TWO, SHIFT_TWO)


def chunk_call(kernel, name, grid, operands, specs, shapes, out_specs, scratch, after=(), far=()):
    first_out = len(operands)
    return pl.pallas_call(
        lambda *refs: kernel(*refs[:first_out], *refs[first_out + len(after) :]),
        grid=(grid,),
        out_shape=tuple(
            pltpu.HBM(shape, kind) if number in far else jax.ShapeDtypeStruct(shape, kind)
            for number, (shape, kind) in enumerate(shapes)
        ),
        in_specs=list(specs) + [pl.BlockSpec(memory_space=pl.ANY)] * len(after),
        out_specs=tuple(out_specs),
        scratch_shapes=scratch,
        compiler_params=pltpu.CompilerParams(vmem_limit_bytes=VMEM_BYTES),
        cost_estimate=FREE,
        name=name,
    )(*operands, *after)


def sent_and_kept(total_ref, part_ref, send_ref):
    @pl.when(pl.program_id(0) == pl.num_programs(0) - 1)
    def _():
        count = part_ref.shape[0]
        part_ref[...] = total_ref[:count, :]
        send_ref[...] = low(total_ref[count:, :])


def take_both(own_ref, other_ref, chip_ref):
    @pl.when(pl.program_id(0) == 0)
    def _():
        count = own_ref.shape[0]
        chip_ref[:count, :] = own_ref[...]
        chip_ref[count:, :] = other_ref[...]


def add_up(total_ref, term):
    @pl.when(pl.program_id(0) == 0)
    def _():
        total_ref[...] = term

    @pl.when(pl.program_id(0) > 0)
    def _():
        total_ref[...] += term


def mlp_kernel(
    own_ref, other_ref, hidden_ref, down_ref, bias_ref, act_ref, slope_ref, part_ref, send_ref, chip_ref, total_ref
):
    take_both(own_ref, other_ref, chip_ref)
    pre = plain_product(chip_ref[...], hidden_ref[...]) + bias_ref[...]
    square = pre * pre
    factor = math.sqrt(2.0 / math.pi)
    bent = jnp.tanh(pre * (factor + (factor * 0.044715) * square))
    near_half = 0.5 + 0.5 * bent
    act = low(pre * near_half)
    act_ref[...] = act
    slope_ref[...] = low(
        near_half
        + (0.5 * pre) * (1.0 - bent * bent) * (factor + (3.0 * factor * 0.044715) * square)
    )
    add_up(total_ref, plain_product(act, down_ref[...]))
    sent_and_kept(total_ref, part_ref, send_ref)


def run_mlp(own, other, hiddens, downs, bias, after):
    count, width = own.shape
    cuts = hiddens.shape[1]
    size = 384
    fixed = lambda rows, columns: pl.BlockSpec((rows, columns), lambda at: (0, 0))
    across = lambda rows: pl.BlockSpec((rows, size), lambda at: (0, at))
    return chunk_call(
        mlp_kernel, "mlp", cuts // size,
        [own, other, hiddens, downs, bias],
        [
            fixed(count, width), fixed(count, width), across(width),
            pl.BlockSpec((size, width), lambda at: (at, 0)), across(1),
        ],
        [
            ((2 * count, cuts), jnp.bfloat16), ((2 * count, cuts), jnp.bfloat16),
            ((count, width), jnp.float32), ((count, width), jnp.bfloat16), ((2 * count, width), jnp.bfloat16),
        ],
        [across(2 * count), across(2 * count), fixed(count, width), fixed(count, width), fixed(2 * count, width)],
        [pltpu.VMEM((2 * count, width), jnp.float32)],
        after,
        (0, 1),
    )


def leave_kernel(last, part_ref, arrived_ref, middle_ref, vec_ref, *refs):
    branch = part_ref[...] + wide(arrived_ref[...]) + row_of(vec_ref, BIAS_DOWN)
    state = middle_ref[...] + row_of(vec_ref, GATE_TWO) * branch
    if last:
        branch_ref, out_ref = refs
        out_ref[...] = low(state)
    else:
        next_vec_ref, branch_ref, state_ref, n_ref = refs
        state_ref[...] = state
        n_ref[...] = norm_rows(state, next_vec_ref, GAIN_ONE, SCALE_ONE, SHIFT_ONE)
    branch_ref[...] = low(branch)


def start_back(grad, branch_ref, vec_ref, d_branch_ref, sums_ref, first):
    d_branch = low(row_of(vec_ref, GATE_TWO) * grad)
    d_branch_ref[...] = d_branch
    sums_ref[first : first + 1, :] = jnp.sum(grad * wide(branch_ref[...]), axis=0, keepdims=True)
    sums_ref[first + 1 : first + 2, :] = jnp.sum(wide(d_branch), axis=0, keepdims=True)


def top_kernel(masked_ref, vec_ref, grad_ref, d_branch_ref):
    grad = wide(masked_ref[...])
    grad_ref[...] = grad
    d_branch_ref[...] = low(row_of(vec_ref, GATE_TWO) * grad)


def top_sums_kernel(grad_ref, d_branch_ref, branch_ref, sums_ref):
    sums_ref[0:1, :] = jnp.sum(grad_ref[...] * wide(branch_ref[...]), axis=0, keepdims=True)
    sums_ref[1:2, :] = jnp.sum(wide(d_branch_ref[...]), axis=0, keepdims=True)


def mlp_back_kernel(
    own_ref, other_ref, slope_ref, hidden_ref, down_ref, d_pre_ref, part_ref, send_ref, bias_ref, chip_ref, total_ref
):
    take_both(own_ref, other_ref, chip_ref)
    d_pre = low(right_product(chip_ref[...], down_ref[...]) * wide(slope_ref[...]))
    d_pre_ref[...] = d_pre
    bias_ref[...] = jnp.sum(wide(d_pre), axis=0, keepdims=True)
    add_up(total_ref, right_product(d_pre, hidden_ref[...]))
    sent_and_kept(total_ref, part_ref, send_ref)


def run_mlp_back(own, other, slope, hiddens, downs, after):
    count, width = own.shape
    cuts = hiddens.shape[1]
    size = 384
    fixed = lambda rows, columns: pl.BlockSpec((rows, columns), lambda at: (0, 0))
    across = lambda rows: pl.BlockSpec((rows, size), lambda at: (0, at))
    return chunk_call(
        mlp_back_kernel, "mlp_back", cuts // size,
        [own, other, pltpu.with_memory_space_constraint(slope, pltpu.HBM), hiddens, downs],
        [
            fixed(count, width), fixed(count, width), across(2 * count), across(width),
            pl.BlockSpec((size, width), lambda at: (at, 0)),
        ],
        [
            ((2 * count, cuts), jnp.bfloat16), ((count, width), jnp.float32), ((count, width), jnp.bfloat16),
            ((1, cuts), jnp.float32), ((2 * count, width), jnp.bfloat16),
        ],
        [across(2 * count), fixed(count, width), fixed(count, width), across(1), fixed(2 * count, width)],
        [pltpu.VMEM((2 * count, width), jnp.float32)],
        after,
    )


def norm_back(d_normed, values, gain, scale, shift_sum_ref):
    unit_values, inverse = normalise(values)
    first = jnp.sum(d_normed, axis=0, keepdims=True)
    second = jnp.sum(d_normed * unit_values, axis=0, keepdims=True)
    shift_sum_ref[0:1, :] = first
    shift_sum_ref[1:2, :] = gain * second
    shift_sum_ref[2:3, :] = (1.0 + scale) * second
    scaled = d_normed * ((1.0 + scale) * gain)
    inner = jnp.mean(scaled * unit_values, axis=-1, keepdims=True)
    return (scaled - jnp.mean(scaled, axis=-1, keepdims=True) - unit_values * inner) * inverse


def middle_back_kernel(
    place_ref, grad_ref, part_ref, arrived_ref, middle_ref, branch_ref, vec_ref, weight_ref,
    d_middle_ref, d_branch_ref, att_own_ref, att_other_ref, sums_ref, d_att_ref,
):
    half = att_own_ref.shape[1]
    d_normed = part_ref[...] + wide(arrived_ref[...])
    d_middle = grad_ref[...] + norm_back(
        d_normed, middle_ref[...], row_of(vec_ref, GAIN_TWO), row_of(vec_ref, SCALE_TWO), sums_ref
    )
    d_middle_ref[...] = d_middle
    sums_ref[3:4, :] = jnp.sum(d_middle * wide(branch_ref[...]), axis=0, keepdims=True)
    d_branch_ref[...] = low(row_of(vec_ref, GATE_ONE) * d_middle)
    d_att_ref[...] = low(right_product(d_branch_ref[...], weight_ref[...]))
    att_own_ref[...] = d_att_ref[:, pl.ds(pl.multiple_of(place_ref[2] * half, 128), half)]
    att_other_ref[...] = d_att_ref[:, pl.ds(pl.multiple_of((1 - place_ref[2]) * half, 128), half)]


def project_back_kernel(d_qkv_ref, weight_ref, part_ref, send_ref):
    count = part_ref.shape[0]
    columns = d_qkv_ref.shape[1]
    part_ref[...] = right_product(d_qkv_ref[:count, :], weight_ref[:, :columns])
    send_ref[...] = low(right_product(d_qkv_ref[count:, :], weight_ref[:, :columns]))


def enter_back_kernel(last, d_middle_ref, part_ref, arrived_ref, state_ref, vec_ref, *refs):
    d_normed = part_ref[...] + wide(arrived_ref[...])
    if last:
        sums_ref, out_ref = refs
    else:
        branch_ref, next_vec_ref, sums_ref, grad_ref, d_branch_ref = refs
    grad = d_middle_ref[...] + norm_back(
        d_normed, wide(state_ref[...]), row_of(vec_ref, GAIN_ONE), row_of(vec_ref, SCALE_ONE), sums_ref
    )
    if last:
        out_ref[...] = low(grad)
    else:
        grad_ref[...] = grad
        start_back(grad, branch_ref, next_vec_ref, d_branch_ref, sums_ref, 3)


def attend_kernel(seg_q_ref, seg_k_ref, q_ref, kl_ref, vl_ref, kf_ref, vf_ref, *refs):
    own_ref, other_ref, lse_ref = refs[-3:]
    count = kl_ref.shape[0]
    TILE = count // 2
    low_half = lax.broadcasted_iota(jnp.int32, (count, 128), 1) < 64
    for start in range(0, q_ref.shape[0], TILE):
        rows = pl.ds(start, TILE)
        seg_q = seg_q_ref[rows, :]
        allow_l = seg_q == seg_k_ref[:, :count]
        allow_f = seg_q == seg_k_ref[:, count:]
        query = q_ref[rows, :]
        query = query * jnp.asarray(0.125, query.dtype)
        outs, lses = [], []
        for head in range(2):
            half = low_half if head == 0 else jnp.logical_not(low_half)
            q_h = jnp.where(half[:TILE], query, jnp.zeros_like(query))
            s_l = jnp.where(allow_l, right_product(q_h, kl_ref[...]), neg_big)
            s_f = jnp.where(allow_f, right_product(q_h, kf_ref[...]), neg_big)
            top = jnp.maximum(
                jnp.max(s_l, axis=1, keepdims=True), jnp.max(s_f, axis=1, keepdims=True)
            )
            p_l = jnp.exp(s_l - top).astype(jnp.bfloat16)
            p_f = jnp.exp(s_f - top).astype(jnp.bfloat16)
            one = jnp.ones((count, 128), jnp.bfloat16)
            summed = plain_product(p_l, jnp.where(half, vl_ref[...], one)) + plain_product(
                p_f, jnp.where(half, vf_ref[...], one)
            )
            total = pltpu.roll(summed, 64, 1)
            outs.append(summed / total)
            lses.append(top + jnp.log(total))
        result = jnp.where(low_half[:TILE], outs[0], outs[1])
        (own_ref if start == 0 else other_ref)[...] = result.astype(jnp.bfloat16)
        lse_ref[rows, :] = jnp.where(low_half[:TILE], lses[0], lses[1])


def attend(query, near, far, seg_q, seg_k, after):
    count, half = query.shape
    pairs = half // 128
    block = lambda off: pl.BlockSpec((count, 128), lambda j: (0, off + j))
    part = pl.BlockSpec((count // 2, 128), lambda j: (0, j))
    return pl.pallas_call(
        attend_kernel,
        grid=(pairs,),
        out_shape=(
            jax.ShapeDtypeStruct((count // 2, half), jnp.bfloat16),
            jax.ShapeDtypeStruct((count // 2, half), jnp.bfloat16),
            pltpu.HBM((count, half), jnp.float32),
        ),
        in_specs=[
            pl.BlockSpec((count, 1), lambda j: (0, 0)),
            pl.BlockSpec((1, 2 * count), lambda j: (0, 0)),
            block(0),
            block(0),
            block(pairs),
            block(0),
            block(pairs),
        ]
        + [pl.BlockSpec(memory_space=pl.ANY)] * len(after),
        out_specs=(part, part, block(0)),
        compiler_params=pltpu.CompilerParams(vmem_limit_bytes=VMEM_BYTES),
        cost_estimate=FREE,
        name="attend",
    )(seg_q, seg_k, query, near, near, far, far, *after)


def back_kernel(has_more, seg_q_ref, seg_k_ref, q_ref, k_ref, v_ref, do_own_ref, do_other_ref, o_own_ref, o_other_ref, lse_ref, *refs):
    count = k_ref.shape[0]
    TILE = count // 2
    low_half = lax.broadcasted_iota(jnp.int32, (TILE, 128), 1) < 64
    q_turned = (q_ref[...].astype(jnp.float32) * 0.125).T.astype(jnp.bfloat16)
    do_turned = [ref[...].astype(jnp.float32).T.astype(jnp.bfloat16) for ref in (do_own_ref, do_other_ref)]
    d_keys, d_values, d_queries = [0.0, 0.0], [0.0, 0.0], []
    for start in range(0, q_ref.shape[0], TILE):
        rows = pl.ds(start, TILE)
        allow = seg_q_ref[rows, :] == seg_k_ref[...]
        query = q_ref[rows, :]
        query = query * jnp.asarray(0.125, query.dtype)
        d_out = (do_own_ref if start == 0 else do_other_ref)[...]
        product = wide(d_out) * wide((o_own_ref if start == 0 else o_other_ref)[...])
        d_query = []
        for head in range(2):
            half = low_half if head == 0 else jnp.logical_not(low_half)
            lanes = slice(64 * head, 64 * head + 64)
            q_h = jnp.where(half, query, jnp.zeros_like(query))
            do_h = jnp.where(half, d_out, jnp.zeros_like(d_out))
            scores = jnp.where(allow, right_product(q_h, k_ref[...]), neg_big)
            probs = jnp.exp(scores - lse_ref[rows, 64 * head : 64 * head + 1])
            d_probs = right_product(do_h, v_ref[...])
            delta = jnp.sum(jnp.where(half, product, 0.0), axis=1, keepdims=True)
            d_scores = (probs * (d_probs - delta)).astype(jnp.bfloat16)
            d_values[head] += plain_product(
                do_turned[start // TILE][lanes], probs.astype(jnp.bfloat16)
            )
            d_keys[head] += plain_product(q_turned[lanes, start : start + TILE], d_scores)
            d_query.append(plain_product(d_scores, k_ref[...]))
        d_queries.append(jnp.where(low_half, d_query[0], d_query[1]) * 0.125)
    d_key = jnp.concatenate(d_keys, axis=0).T
    d_value = jnp.concatenate(d_values, axis=0).T
    d_query = jnp.concatenate(d_queries, axis=0)
    if has_more:
        dq_more_ref, dk_more_ref, dv_more_ref, out_ref = refs
        half = out_ref.shape[1] // 3
        at = pl.multiple_of(pl.program_id(0) * 128, 128)
        out_ref[:, pl.ds(at, 128)] = (d_query + dq_more_ref[...]).astype(jnp.bfloat16)
        out_ref[:, pl.ds(half + at, 128)] = (d_key + dk_more_ref[...].astype(jnp.float32)).astype(
            jnp.bfloat16
        )
        out_ref[:, pl.ds(2 * half + at, 128)] = (
            d_value + dv_more_ref[...].astype(jnp.float32)
        ).astype(jnp.bfloat16)
    else:
        dq_ref, out_ref = refs
        half = out_ref.shape[1] // 2
        at = pl.multiple_of(pl.program_id(0) * 128, 128)
        dq_ref[...] = d_query
        out_ref[:, pl.ds(at, 128)] = d_key.astype(jnp.bfloat16)
        out_ref[:, pl.ds(half + at, 128)] = d_value.astype(jnp.bfloat16)


def attend_back(query, keys, seg_q, seg_k, d_outs, out, lse, more=None, after=()):
    count, half = query.shape
    pairs = half // 128
    block = lambda off: pl.BlockSpec((count, 128), lambda j: (0, off + j))
    part = pl.BlockSpec((count // 2, 128), lambda j: (0, j))
    whole = lambda width: pl.BlockSpec((count, width), lambda j: (0, 0))
    operands = [seg_q, seg_k, query, keys, keys, *d_outs, *out]
    operands.append(pltpu.with_memory_space_constraint(lse, pltpu.HBM))
    specs = [
        pl.BlockSpec((count, 1), lambda j: (0, 0)),
        pl.BlockSpec((1, count), lambda j: (0, 0)),
        block(0),
        block(0),
        block(pairs),
        part,
        part,
        part,
        part,
        block(0),
    ]
    if more is None:
        out_shape = (
            jax.ShapeDtypeStruct((count, half), jnp.float32),
            jax.ShapeDtypeStruct((count, 2 * half), jnp.bfloat16),
        )
        out_specs = (block(0), whole(2 * half))
    else:
        operands += [more[0], more[1], more[1]]
        specs += [block(0), block(0), block(pairs)]
        out_shape = jax.ShapeDtypeStruct((count, 3 * half), jnp.bfloat16)
        out_specs = whole(3 * half)
    first_out = len(operands)
    operands += after
    specs += [pl.BlockSpec(memory_space=pl.ANY)] * len(after)
    return pl.pallas_call(
        lambda *refs: back_kernel(more is not None, *refs[:first_out], *refs[first_out + len(after) :]),
        grid=(pairs,),
        out_shape=out_shape,
        in_specs=specs,
        out_specs=out_specs,
        compiler_params=pltpu.CompilerParams(vmem_limit_bytes=VMEM_BYTES),
        cost_estimate=FREE,
        name="attend_back",
    )(*operands)


def local_paired(
    tokens,
    cotangent,
    segments,
    noised,
    levels,
    ada_weight,
    ada_bias,
    first_gain,
    qkv_weight,
    out_weight,
    second_gain,
    hidden_weight,
    hidden_bias,
    down_weight,
    down_bias,
):
    layers, ada_part, cond_width = ada_weight.shape
    part = first_gain.shape[1]
    hidden_part = hidden_bias.shape[1]
    width = tokens.shape[2]
    shards = width // part
    hidden = hidden_part * shards
    half = width // 2
    rows_in = part // 4
    rows_down = hidden_part // 8
    hidden_cut = hidden_part // 2
    blk = lax.axis_index("blk")
    uly = lax.axis_index("uly")
    core = uly // 2
    side = uly % 2
    quarter = blk * 2 + side
    shard = lax.axis_index("dp")
    row = shard * 2 + blk
    place = jnp.stack([shard, quarter, core]).astype(jnp.int32)

    def exchange(two_rows):
        return jnp.concatenate(
            [pick(two_rows, blk, 0), swap_blk(pick(two_rows, 1 - blk, 0))], axis=0
        )

    sizes = (rows_in, rows_down, half, hidden_cut, shards)
    qkv_weight, out_weight, hidden_weight, down_weight = (
        pltpu.with_memory_space_constraint(weight, pltpu.HBM)
        for weight in (qkv_weight, out_weight, hidden_weight, down_weight)
    )
    columns = 4 * half
    attn_columns = 3 * half
    mlp_columns = 5 * half

    def spread(own, last):
        near, far = swap_half(own), swap_blk(own)
        return (own, near, far, swap_blk(near) if last == "blk" else swap_half(far))

    def cut_attn(index, after):
        return copy_call(
            lambda *refs: cut_attn_kernel(sizes, index, *refs), "cut_attn", place,
            [qkv_weight], [(rows_in, attn_columns)], 3, after,
        )[0]

    def cut_mlp(index, after):
        return copy_call(
            lambda *refs: cut_mlp_kernel(sizes, index, *refs), "cut_mlp", place,
            [out_weight, hidden_weight, down_weight], [(2 * rows_in, mlp_columns)], shards + 4, after,
        )[0]

    def cut_next(index, after):
        return copy_call(
            lambda *refs: cut_next_kernel(sizes, index, *refs), "cut_next", place,
            [qkv_weight, out_weight, hidden_weight, down_weight],
            [(3 * rows_in, mlp_columns)], shards + 7, after,
        )[0]

    def whole_attn(index, spread):
        joined = copy_call(
            lambda *refs: join_attn_kernel(sizes, index, *refs), "join_attn", place,
            [qkv_weight, *spread], [(shards, part, attn_columns)], 3 + 4 * (shards - 1), (), True,
        )[0]
        return joined.reshape(width, attn_columns)

    def whole_mlp(index, spread):
        outs, hiddens, downs = copy_call(
            lambda *refs: join_mlp_kernel(sizes, index, *refs), "join_mlp", place,
            [out_weight, hidden_weight, down_weight, *spread],
            [(shards, part, width), (shards, part, columns), (shards, hidden_cut, width)],
            shards + 2 + 20 * (shards - 1), (), True,
        )
        return (
            outs.reshape(width, width), hiddens.reshape(width, columns),
            downs.reshape(shards * hidden_cut, width),
        )

    start = exchange(tokens)
    segs_two = exchange(segments)
    seg_chip = jnp.concatenate([segs_two, swap_core(segs_two)])
    seg_far = swap_half(seg_chip)
    def every_shard_of(piece):
        return lax.all_gather(piece, "dp", axis=0, tiled=False)

    def others_of(piece):
        return jnp.stack([from_shard(piece, back, shards) for back in range(1, shards)])

    def every_shard(vector):
        table = jnp.stack([vector] + [from_shard(vector, back, shards) for back in range(1, shards)])
        return jnp.stack([pick(table, (shard + shards - at) % shards, 0) for at in range(shards)])

    all_levels = every_shard(levels)
    attn_piece = cut_attn(0, [])
    attn_own = others_of(attn_piece)
    attn = spread(attn_own, "half")
    mlp_piece = cut_mlp(0, [attn_own])
    mlp_whole = every_shard_of(mlp_piece)
    next_whole = [every_shard_of(cut_next(index, [mlp_piece])) for index in range(1, layers)]

    all_levels = all_levels.reshape(-1)
    conds = low(cond_vector(all_levels, cond_width))
    part_mods = jnp.stack(
        [right_product(conds, ada_weight[index]) + wide(ada_bias[index]) for index in range(layers)],
        axis=1,
    )
    own_vectors = wide(
        jnp.concatenate([first_gain, second_gain, down_bias, hidden_bias], axis=1)
    )

    def shared_for(target):
        return jnp.concatenate([pick(part_mods, target * 2 + blk, 0), own_vectors], axis=1)

    shared = [shared_for(shard)]
    for ahead in range(1, shards):
        shared.append(from_shard(shared_for((shard + ahead) % shards), ahead, shards))
    shared = jnp.stack(shared)
    shared = jnp.stack([pick(shared, (shard + shards - at) % shards, 0) for at in range(shards)])
    vectors = []
    for index in range(layers):
        table = shared[:, index]
        ends = [ada_part + number * part for number in range(4)]
        rows = [table[:, :ada_part].reshape(6, width)]
        rows += [table[:, first : first + part].reshape(1, width) for first in ends[:3]]
        bias_hidden = table[:, ends[3] :].reshape(shards, 2, hidden_cut)
        vectors.append(
            (jnp.concatenate(rows, axis=0), pick(bias_hidden, core, 1).reshape(1, shards * hidden_cut))
        )

    seg_q = seg_chip[:, None]
    seg_near_k, seg_far_k = seg_chip[None, :], seg_far[None, :]
    seg_k = jnp.concatenate([seg_near_k, seg_far_k], axis=1)

    def spread_late(own, after):
        near, far = swap_half(own), hold(swap_blk(own), after)
        return (own, near, far, swap_half(far))

    tokens_here = start.shape[0]
    rows_f32 = ((tokens_here, width), jnp.float32)
    rows_low = ((tokens_here, width), jnp.bfloat16)
    half_low = ((tokens_here, half), jnp.bfloat16)
    chip_low = ((2 * tokens_here, width), jnp.bfloat16)
    cut_wide = shards * hidden_cut
    state = wide(start)
    normed = whole_call(
        enter_kernel, "enter", [rows_low], [start, vectors[0][0]], None, [seg_far]
    )[0]
    masked = exchange(cotangent * low(noised)[..., None])
    grad, d_branch_two = whole_call(top_kernel, "top", [rows_f32, rows_low], [masked, vectors[-1][0]])
    d_branch_other = swap_core(d_branch_two)
    kept, gathered = [], []
    for index in range(layers):
        vec, bias_core = vectors[index]
        joined = whole_attn(index, attn)
        normed_other = swap_core(normed)
        near, normed_chip = whole_call(
            lambda *refs: project_kernel(half, 3 * half, *refs), "keys_values",
            [((2 * tokens_here, 2 * half), jnp.bfloat16), chip_low], [normed, normed_other, joined],
        )
        far = swap_half(near)
        query = whole_call(
            lambda *refs: project_kernel(0, half, *refs), "queries",
            [((2 * tokens_here, half), jnp.bfloat16)], [normed, normed_other, joined], None, [near],
        )[0]
        att_own, att_send, lse = attend(query, near, far, seg_q, seg_k, ())
        att_other = swap_core(att_send)
        if index == 0:
            mlp_own = others(place, mlp_whole, [(0, 2 * rows_in, mlp_columns)], [att_own])[0]
        mlp = spread_late(mlp_own, att_other)
        out_whole, hiddens, downs = whole_mlp(index, mlp)
        gathered.append((hiddens, downs))
        branch_one, middle, normed_two, attended = whole_call(
            middle_kernel, "middle", [rows_low, rows_f32, rows_low, rows_low],
            [att_own, att_other, out_whole, state, vec], place,
        )
        normed_two_other = swap_core(normed_two)
        after = [d_branch_other] if index == layers - 1 else []
        act, slope, part_own, part_send, normed_two_chip = run_mlp(
            normed_two, normed_two_other, hiddens, downs, bias_core, after
        )
        if index + 1 < layers:
            mlp_own, attn_own = others(
                place, next_whole[index],
                [(0, 2 * rows_in, mlp_columns), (2 * rows_in, rows_in, attn_columns)], [part_own],
            )
            attn = spread(attn_own, "half")
        ends = [part_own, swap_core(part_send), middle, vec]
        keep = [
            state, normed_chip, joined, out_whole, query, near, far, (att_own, att_send), lse, attended,
            branch_one, middle, normed_two_chip, act, slope,
        ]
        if index == layers - 1:
            branch_two, final = whole_call(
                lambda *refs: leave_kernel(True, *refs), "leave", [rows_low, rows_low], ends
            )
        else:
            branch_two, state, normed = whole_call(
                lambda *refs: leave_kernel(False, *refs), "leave", [rows_low, rows_f32, rows_low],
                ends + [vectors[index + 1][0]], None, (),
            )
        kept.append(keep + [branch_two])

    def give_back(rows):
        mine, other = rows[: rows.shape[0] // 2], rows[rows.shape[0] // 2 :]
        arrived = swap_blk(other)
        return jnp.where(blk == 0, jnp.stack([mine, arrived]), jnp.stack([arrived, mine]))

    output = give_back(final)

    def reduce_start(array, rows):
        terms = array.reshape(shards, 2, 2, rows, array.shape[1])
        first = swap_half(pick(terms, 1 - side, 2))
        kept_terms = low(wide(pick(terms, side, 2)) + wide(first))
        return pick(kept_terms, blk, 1), swap_blk(pick(kept_terms, 1 - blk, 1))

    def reduce_end(pair, *after):
        mine, arrived = pair
        return low(wide(mine) + wide(hold(arrived, *after) if after else arrived))

    def scatter_shards(array):
        return lax.psum_scatter(array, "dp", scatter_dimension=0, tiled=False)

    def sum_shards(array):
        arrived = [
            from_shard(pick(array, (shard + ahead) % shards, 0), ahead, shards)
            for ahead in range(1, shards)
        ]
        return low(wide(pick(array, shard, 0)) + sum(wide(item) for item in arrived)), arrived[0]

    sums_top = whole_call(
        top_sums_kernel, "top_sums", [((2, width), jnp.float32)], [grad, d_branch_two, kept[-1][-1]]
    )[0]
    def end_mlp_sums(pending, late):
        index, down_pair, hidden_pair, _, _ = pending
        down_sum, hidden_sum = reduce_end(down_pair, late), reduce_end(hidden_pair, late)
        down_sum = jnp.concatenate([down_sum[:, :rows_in], down_sum[:, rows_in:]], axis=2)
        return scatter_shards(jnp.concatenate([hidden_sum, down_sum], axis=1))

    def end_attn_sums(pending, late):
        index, _, _, attn_pair, out_sum = pending
        attn_sum = reduce_end(attn_pair, late) if index > 0 else reduce_end(attn_pair)
        attn_sum = jnp.concatenate([attn_sum, out_sum], axis=2)
        return (scatter_shards(attn_sum), None) if index > 0 else sum_shards(attn_sum)

    pending = None
    small = [None] * layers
    shards_out = [None] * layers
    due = [()] * 5
    for index in reversed(range(layers)):
        vec, _ = vectors[index]
        hiddens, downs = gathered[index]
        (
            state_in, normed_chip, joined, out_whole, query, near, far, heads_out, lse, attended,
            branch_one, middle, normed_two_chip, act, slope, _,
        ) = kept[index]
        if index < layers - 1:
            d_branch_other = swap_core(d_branch_two)
        d_pre, part_own, part_send, d_bias_core, d_branch_chip = run_mlp_back(
            d_branch_two, d_branch_other, slope, hiddens, downs, due[0]
        )
        if pending is not None:
            shards_out[pending[0]] = (None, end_mlp_sums(pending, d_pre))
        d_down = low(left_product(act, d_branch_chip))
        d_hidden = low(left_product(normed_two_chip, d_pre))
        down_pair, hidden_pair = reduce_start(d_down, rows_down), reduce_start(d_hidden, rows_in)
        d_middle, d_one, d_att_own, d_att_send, sums_middle, _ = whole_call(
            middle_back_kernel, "middle_back",
            [rows_f32, rows_low, half_low, half_low, ((4, width), jnp.float32), rows_low],
            [grad, part_own, swap_core(part_send), middle, branch_one, vec, out_whole], place, due[1],
        )
        d_heads = (d_att_own, swap_core(d_att_send))
        d_query_far, d_far = attend_back(
            query, far, seg_q, seg_far_k, d_heads, heads_out, lse, None, due[2],
        )
        if pending is not None:
            shards_out[pending[0]] = (end_attn_sums(pending, d_query_far)[0], shards_out[pending[0]][1])
        d_near = swap_half(d_far)
        out_sum = reduce_end(reduce_start(low(left_product(attended, d_one)), rows_in))
        out_sum = low(
            wide(lax.dynamic_slice_in_dim(out_sum, core * half, half, 2))
            + wide(swap_core(lax.dynamic_slice_in_dim(out_sum, (1 - core) * half, half, 2)))
        )
        d_qkv = attend_back(
            query, near, seg_q, seg_near_k, d_heads, heads_out, lse, (d_query_far, d_near),
            due[3],
        )
        d_qkv_core = low(left_product(normed_chip, d_qkv))
        attn_pair = reduce_start(d_qkv_core, rows_in)
        part_own, part_send = whole_call(
            project_back_kernel, "project_back", [rows_f32, rows_low], [d_qkv, joined], None, due[4]
        )
        ends = [d_middle, part_own, swap_core(part_send), state_in, vec]
        sums_next = None
        if index == 0:
            sums_in, last_grad = whole_call(
                lambda *refs: enter_back_kernel(True, *refs), "enter_back",
                [((3, width), jnp.float32), rows_low], ends,
            )
        else:
            sums_in, grad, d_branch_two = whole_call(
                lambda *refs: enter_back_kernel(False, *refs), "enter_back",
                [((5, width), jnp.float32), rows_f32, rows_low],
                ends + [kept[index - 1][-1], vectors[index - 1][0]], None,
                (),
            )
            sums_next = sums_in[3:]
        pending = (index, down_pair, hidden_pair, attn_pair, out_sum)
        d_units = d_bias_core.reshape(shards, 1, hidden_cut)
        d_units = jnp.concatenate(
            [jnp.where(core == 0, d_units, 0.0), jnp.where(core == 1, d_units, 0.0)], axis=1
        )
        d_modulation = jnp.concatenate(
            [sums_in[:2], sums_middle[3:4], sums_middle[:2], sums_top[:1]], axis=0
        )
        small[index] = jnp.concatenate(
            [
                d_modulation.reshape(shards, -1),
                sums_in[2].reshape(shards, -1),
                sums_middle[2].reshape(shards, -1),
                sums_top[1].reshape(shards, -1),
                d_units.reshape(shards, -1),
            ],
            axis=1,
        )
        sums_top = sums_next

    attn_shard, shard_arrived = end_attn_sums(pending, None)
    shards_out[0] = (attn_shard, end_mlp_sums(pending, last_grad))
    tokens_grad = give_back(last_grad)

    vector = jnp.stack(small)
    vector = vector + swap_core(vector)
    vector = vector + swap_half(vector)
    parts = vector.transpose(1, 0, 2)
    arrived = [pick(parts, shard, 0)]
    for ahead in range(1, shards):
        arrived.append(from_shard(pick(parts, (shard + ahead) % shards, 0), ahead, shards))
    arrived = jnp.stack(arrived)
    other = swap_blk(arrived)
    totals = jnp.sum(arrived + other, axis=0)
    cond_rows = wide(conds).reshape(shards, 2, cond_width)
    cond_rows = jnp.stack([pick(cond_rows, (shard + shards - at) % shards, 0) for at in range(shards)])
    by_row = jnp.concatenate([arrived[:, :, :ada_part], other[:, :, :ada_part]], axis=0)
    cond_both = jnp.concatenate([pick(cond_rows, blk, 1), pick(cond_rows, 1 - blk, 1)], axis=0)
    grad_ada = jnp.einsum(
        "slm,sc->lmc", by_row, cond_both, precision=lax.Precision.HIGHEST
    )
    grad_ada_bias = totals[:, :ada_part]
    at = ada_part
    grad_gain_one = totals[:, at : at + part]
    grad_gain_two = totals[:, at + part : at + 2 * part]
    grad_bias_down = totals[:, at + 2 * part : at + 3 * part]
    grad_bias_hidden = totals[:, at + 3 * part :]

    def every_piece(piece, after):
        far, across = swap_blk(piece), swap_core(piece)
        cut = 4 * rows_in // 3
        last = jnp.concatenate([swap_blk(across[:cut]), swap_core(far[cut:])], axis=0)
        mine = jnp.stack([piece, far, across, last])
        other = swap_half(hold(mine, after) if after is not None else mine)
        return (
            jnp.stack([mine[0], other[0], mine[1], other[1]]),
            jnp.stack([mine[2], other[2], mine[3], other[3]]),
        )

    shapes = {
        "attn": [(layers, part, 3 * width), (layers, part, width)],
        "mlp": [(layers, part, hidden), (layers, 2, 4, rows_down, width)],
    }
    grads = None
    for index in reversed(range(layers)):
        piece = jnp.concatenate(shards_out[index], axis=0)
        if index > 0:
            piece = hold(piece, token(shard_arrived))
        grads = finish(
            place, index, ("attn", "mlp"), every_piece(piece, None), shapes, half, rows_in, shards, grads
        )
    grad_qkv, grad_out, grad_hidden, grad_down = grads
    grad_down = grad_down.reshape(layers, hidden_part, width)
    return (
        output,
        tokens_grad,
        grad_ada,
        grad_ada_bias,
        grad_gain_one,
        grad_qkv,
        grad_out,
        grad_gain_two,
        grad_hidden,
        grad_bias_hidden,
        grad_down,
        grad_bias_down,
    )


def pick_plan(mesh):
    def run(*arrays):
        tokens, first_gain, hidden_bias = arrays[0], arrays[7], arrays[12]
        fits = (
            mesh.shape["blk"] == 2
            and mesh.shape["uly"] == 4
            and tokens.shape[0] == 2
            and tokens.shape[1] % 64 == 0
            and tokens.shape[2] == HEADS * 64
            and HEADS % 4 == 0
            and first_gain.shape[1] % 64 == 0
            and hidden_bias.shape[1] % 256 == 0
        )
        return (local_paired if fits else local)(*arrays)

    return run


def solution(mesh):
    in_specs = (
        P("dp", ("blk", "uly"), None),
        P("dp", ("blk", "uly"), None),
        P("dp", ("blk", "uly")),
        P("dp", ("blk", "uly")),
        P("dp"),
        P(None, "dp", None),
        P(None, "dp"),
        P(None, "dp"),
        P(None, "dp", None),
        P(None, "dp", None),
        P(None, "dp"),
        P(None, "dp", None),
        P(None, "dp"),
        P(None, "dp", None),
        P(None, "dp"),
    )
    out_specs = (
        P("dp", ("blk", "uly"), None),
        P("dp", ("blk", "uly"), None),
        P(None, "dp", None),
        P(None, "dp"),
        P(None, "dp"),
        P(None, "dp", None),
        P(None, "dp", None),
        P(None, "dp"),
        P(None, "dp", None),
        P(None, "dp"),
        P(None, "dp", None),
        P(None, "dp"),
    )
    return jax.shard_map(pick_plan(mesh), mesh=mesh, in_specs=in_specs, out_specs=out_specs, check_vma=False)
```

profile of v0, /device:TPU:0, one launch (start us, length us, event | category | flops | bytes accessed | tf_op | source)
XLA Modules:
  0.0 508.3 jit_solution(8191541878045916721)
XLA Ops:
  7.3 5.1 %collective-permute-start.6 = (s32[2]{0:T(128)}, s32[2]{0:T(128)S(1)}, u32[]{:S(2)}, u32[]{:S(2)}) collective-permute-start(s32[2]{0:T(128)} %param.19), channel_id=1, source_target_pairs={{0,24},{8,0},{16,8},{24,16},{1,25},{9,1},{17,9},{25,17},{2,26},{10... | collective-permute-start | bytes 32 | tf_op jit(solution)/shard_map/ppermute | solution.py:488
  14.9 2.9 collective-permute-start.13
  32.7 2.3 collective-permute-done.11
  35.1 2.4 cut_mlp.1.refs_5_
  42.2 4.1 collective-permute-done.15.refs_4_
  47.9 2.6 join_attn.2
  57.1 9.0 %attend.2 = (bf16[256,384]{1,0:T(8,128)(2,1)S(1)}, bf16[256,384]{1,0:T(8,128)(2,1)S(1)}, f32[512,384]{1,0:T(8,128)}) custom-call(s32[512,1]{1,0:T(8,128)S(1)} %copy.44.seg_q_ref.refs_0_, s32[1,1024]{1,0:T(1,128)S(1)} %pad_add_fusion.seg_k_ref, bf16[512,384]{1,0:T(8,128)(2,1)S(1)} %queries.2.q_ref.refs_2_, ...), custom_call_target="tpu_custom_call" | custom-call | tf_op jit(solution)/shard_map/attend/pallas_call | solution.py:1088
  67.6 3.3 all-gather.5.cloned.1.call-done
  76.3 4.2 collective-permute-done.18.refs_1_.refs_2_
  80.5 18.3 %collective-permute-done.20.refs_0_ = bf16[3,96,1920]{2,1,0:T(8,128)(2,1)} collective-permute-done((bf16[3,96,1920]{2,1,0:T(8,128)(2,1)S(1)}, bf16[3,96,1920]{2,1,0:T(8,128)(2,1)}, u32[]{:S(2)}, u32[]{:S(2)}) %collective-permute-start.20) | collective-permute-done | bytes 1105952 | tf_op jit(solution)/shard_map/ppermute | solution.py:476
  98.9 2.9 collective-permute-done.21.refs_7_
  101.9 3.4 join_mlp.2
  113.9 9.1 %collective-permute-done.22.refs_1_ = bf16[256,768]{1,0:T(8,128)(2,1)S(1)} collective-permute-done((bf16[256,768]{1,0:T(8,128)(2,1)}, bf16[256,768]{1,0:T(8,128)(2,1)S(1)}, u32[]{:S(2)}, u32[]{:S(2)}) %collective-permute-start.22) | collective-permute-done | bytes 393248 | tf_op jit(solution)/shard_map/ppermute | solution.py:484
  128.0 8.1 %mlp.2 = (bf16[512,1536]{1,0:T(8,128)(2,1)}, bf16[512,1536]{1,0:T(8,128)(2,1)}, f32[256,768]{1,0:T(8,128)S(1)}, bf16[256,768]{1,0:T(8,128)(2,1)}, bf16[512,768]{1,0:T(8,128)(2,1)S(1)}) custom-call(bf16[256,768]{1,0:T(8,128)(2,1)} %get-tuple-element.100.refs_0_, bf16[256,768]{1,0:T(8,128)(2,1)S(1)} %copy-done.95, bf16[768,1536]{1,0:T(8,128)(2,1)S(1)} %bitcast.268, ...), custom_call_target="tpu_custom_call" | custom-call | tf_op jit(solution)/shard_map/mlp/pallas_call | solution.py:846
  140.2 2.2 others.3
  144.4 3.3 collective-permute-done.23.refs_1_
  153.4 2.2 join_attn.3
  155.6 2.9 collective-permute-done.24.refs_1_
  162.5 8.6 %attend.3 = (bf16[256,384]{1,0:T(8,128)(2,1)S(1)}, bf16[256,384]{1,0:T(8,128)(2,1)S(1)}, f32[512,384]{1,0:T(8,128)}) custom-call(s32[512,1]{1,0:T(8,128)S(1)} %copy-done.5, s32[1,1024]{1,0:T(1,128)S(1)} %pad_add_fusion.seg_k_ref, bf16[512,384]{1,0:T(8,128)(2,1)S(1)} %queries.3.q_ref.refs_2_, ...), custom_call_target="tpu_custom_call" | custom-call | tf_op jit(solution)/shard_map/attend/pallas_call | solution.py:1088
  174.0 4.7 collective-permute-done.31.refs_0_
  184.4 4.6 collective-permute-done.34
  192.6 3.9 join_mlp.3
  202.0 8.5 %collective-permute-done.33.refs_1_ = bf16[256,768]{1,0:T(8,128)(2,1)S(1)} collective-permute-done((bf16[256,768]{1,0:T(8,128)(2,1)S(1)}, bf16[256,768]{1,0:T(8,128)(2,1)S(1)}, u32[]{:S(2)}, u32[]{:S(2)}) %collective-permute-start.33) | collective-permute-done | bytes 393248 | tf_op jit(solution)/shard_map/ppermute | solution.py:484
  210.5 7.1 %mlp.3 = (bf16[512,1536]{1,0:T(8,128)(2,1)}, bf16[512,1536]{1,0:T(8,128)(2,1)}, f32[256,768]{1,0:T(8,128)S(1)}, bf16[256,768]{1,0:T(8,128)(2,1)}, bf16[512,768]{1,0:T(8,128)(2,1)S(1)}) custom-call(bf16[256,768]{1,0:T(8,128)(2,1)S(1)} %get-tuple-element.114.refs_0_, bf16[256,768]{1,0:T(8,128)(2,1)S(1)} %collective-permute-done.33.refs_1_, ...), custom_call_target="tpu_custom_call" | custom-call | tf_op jit(solution)/shard_map/mlp/pallas_call | solution.py:846
  220.7 6.8 %mlp_back.2 = (bf16[512,1536]{1,0:T(8,128)(2,1)S(1)}, f32[256,768]{1,0:T(8,128)S(1)}, bf16[256,768]{1,0:T(8,128)(2,1)}, f32[1,1536]{1,0:T(1,128)S(1)}, bf16[512,768]{1,0:T(8,128)(2,1)S(1)}) custom-call(bf16[256,768]{1,0:T(8,128)(2,1)S(1)} %get-tuple-element.117.refs_0_.refs_1_, bf16[256,768]{1,0:T(8,128)(2,1)S(1)} %collective-permute-done.35.refs_5_.refs_1_, ...), custom_call_target="tpu_custom_call" | custom-call | tf_op jit(solution)/shard_map/mlp_back/pallas_call | solution.py:846
  233.6 3.0 convolution_convert_fusion
  244.6 3.0 middle_back.2
  266.7 7.0 %attend_back.4 = (f32[512,384]{1,0:T(8,128)S(1)}, bf16[512,768]{1,0:T(8,128)(2,1)S(1)}) custom-call(s32[512,1]{1,0:T(8,128)S(1)} %copy-done.6, s32[1,512]{1,0:T(1,128)S(1)} %bitcast.283, bf16[512,384]{1,0:T(8,128)(2,1)S(1)} %copy-done.23, bf16[512,768]{1,0:T(8,128)(2,1)S(1)} %copy-done.10, bf16[512,768]{1,0:T(8,128)(2,1)S(1)} %copy-done.10, ...), custom_call_target="tpu_custom_call" | custom-call | tf_op jit(solution)/shard_map/attend_back/pallas_call | solution.py:1201
  286.6 7.1 %attend_back.5.refs_0_ = bf16[512,1152]{1,0:T(8,128)(2,1)S(1)} custom-call(s32[512,1]{1,0:T(8,128)S(1)} %copy-done.7, s32[1,512]{1,0:T(1,128)S(1)} %bitcast.280, bf16[512,384]{1,0:T(8,128)(2,1)S(1)} %copy-done.24, bf16[512,768]{1,0:T(8,128)(2,1)S(1)} %copy-done.3, bf16[512,768]{1,0:T(8,128)(2,1)S(1)} %copy-done.3, bf16[256,384]{1,0:T(8,128)(2,1)S(1)} %copy-done.77, ...), custom_call_target="tpu_custom_call" | custom-call | tf_op jit(solution)/shard_map/attend_back/pallas_call | solution.py:1201
  299.0 5.8 %collective-permute-done.41.refs_2_ = bf16[256,768]{1,0:T(8,128)(2,1)S(1)} collective-permute-done((bf16[256,768]{1,0:T(8,128)(2,1)S(1)}, bf16[256,768]{1,0:T(8,128)(2,1)S(1)}, u32[]{:S(2)}, u32[]{:S(2)}) %collective-permute-start.41) | collective-permute-done | bytes 393248 | tf_op jit(solution)/shard_map/ppermute | solution.py:484
  308.2 9.2 %collective-permute-done.42.refs_1_ = bf16[256,768]{1,0:T(8,128)(2,1)S(1)} collective-permute-done((bf16[256,768]{1,0:T(8,128)(2,1)S(1)}, bf16[256,768]{1,0:T(8,128)(2,1)S(1)}, u32[]{:S(2)}, u32[]{:S(2)}) %collective-permute-start.42) | collective-permute-done | bytes 393248 | tf_op jit(solution)/shard_map/ppermute | solution.py:484
  320.7 7.1 %mlp_back.3 = (bf16[512,1536]{1,0:T(8,128)(2,1)S(1)}, f32[256,768]{1,0:T(8,128)S(1)}, bf16[256,768]{1,0:T(8,128)(2,1)}, f32[1,1536]{1,0:T(1,128)S(1)}, bf16[512,768]{1,0:T(8,128)(2,1)S(1)}) custom-call(bf16[256,768]{1,0:T(8,128)(2,1)S(1)} %get-tuple-element.137.refs_0_, bf16[256,768]{1,0:T(8,128)(2,1)S(1)} %collective-permute-done.42.refs_1_, ...), custom_call_target="tpu_custom_call" | custom-call | tf_op jit(solution)/shard_map/mlp_back/pallas_call | solution.py:846
  342.9 2.5 middle_back.3
  347.6 4.6 collective-permute-done.44.refs_6_
  352.2 6.9 %attend_back.6 = (f32[512,384]{1,0:T(8,128)S(1)}, bf16[512,768]{1,0:T(8,128)(2,1)S(1)}) custom-call(s32[512,1]{1,0:T(8,128)S(1)} %copy-done.8, s32[1,512]{1,0:T(1,128)S(1)} %bitcast.284, bf16[512,384]{1,0:T(8,128)(2,1)S(1)} %copy-done.21, bf16[512,768]{1,0:T(8,128)(2,1)} %collective-permute-done.17.kf_ref.vf_ref.refs_3_.refs_4_, ...), custom_call_target="tpu_custom_call" | custom-call | tf_op jit(solution)/shard_map/attend_back/pallas_call | solution.py:1201
  382.0 7.4 %attend_back.7.refs_0_ = bf16[512,1152]{1,0:T(8,128)(2,1)S(1)} custom-call(s32[512,1]{1,0:T(8,128)S(1)} %copy-done.8, s32[1,512]{1,0:T(1,128)S(1)} %bitcast.281, bf16[512,384]{1,0:T(8,128)(2,1)S(1)} %copy-done.21, bf16[512,768]{1,0:T(8,128)(2,1)S(1)} %copy-done.1, bf16[512,768]{1,0:T(8,128)(2,1)S(1)} %copy-done.1, bf16[256,384]{1,0:T(8,128)(2,1)S(1)} %copy-done.74, ...), custom_call_target="tpu_custom_call" | custom-call | tf_op jit(solution)/shard_map/attend_back/pallas_call | solution.py:1201
  393.8 6.2 %collective-permute-done.46.refs_2_ = bf16[256,768]{1,0:T(8,128)(2,1)S(1)} collective-permute-done((bf16[256,768]{1,0:T(8,128)(2,1)S(1)}, bf16[256,768]{1,0:T(8,128)(2,1)S(1)}, u32[]{:S(2)}, u32[]{:S(2)}) %collective-permute-start.46) | collective-permute-done | bytes 393248 | tf_op jit(solution)/shard_map/ppermute | solution.py:484
  412.5 9.1 %collective-permute-done.55 = bf16[4,48,1152]{2,1,0:T(8,128)(2,1)S(1)} collective-permute-done((bf16[4,48,1152]{2,1,0:T(8,128)(2,1)S(1)}, bf16[4,48,1152]{2,1,0:T(8,128)(2,1)S(1)}, u32[]{:S(2)}, u32[]{:S(2)}) %collective-permute-start.55) | collective-permute-done | bytes 442400 | tf_op jit(solution)/shard_map/ppermute | solution.py:476
  424.9 7.3 %collective-permute-done.59 = bf16[48,1536]{1,0:T(8,128)(2,1)S(1)} collective-permute-done((bf16[48,1536]{1,0:T(8,128)(2,1)S(1)}, bf16[48,1536]{1,0:T(8,128)(2,1)S(1)}, u32[]{:S(2)}, u32[]{:S(2)}) %collective-permute-start.59) | collective-permute-done | bytes 147488 | tf_op jit(solution)/shard_map/ppermute | solution.py:488
  435.0 3.7 collective-permute-start.61
  443.2 5.9 %collective-permute-done.61 = bf16[48,1536]{1,0:T(8,128)(2,1)S(1)} collective-permute-done((bf16[48,1536]{1,0:T(8,128)(2,1)S(1)}, bf16[48,1536]{1,0:T(8,128)(2,1)S(1)}, u32[]{:S(2)}, u32[]{:S(2)}) %collective-permute-start.61) | collective-permute-done | bytes 147488 | tf_op jit(solution)/shard_map/ppermute | solution.py:488
  449.1 7.1 %collective-permute-done.60 = bf16[48,1536]{1,0:T(8,128)(2,1)S(1)} collective-permute-done((bf16[48,1536]{1,0:T(8,128)(2,1)S(1)}, bf16[48,1536]{1,0:T(8,128)(2,1)S(1)}, u32[]{:S(2)}, u32[]{:S(2)}) %collective-permute-start.60) | collective-permute-done | bytes 147488 | tf_op jit(solution)/shard_map/ppermute | solution.py:488
  459.5 4.7 collective-permute-done.82
  466.0 3.4 collective-permute-done.66
  485.2 2.5 collective-permute-done.53
  489.1 3.0 fusion.39
  493.4 3.7 finish.2
  497.7 3.7 finish.3
  (697 shorter events, 235.5 us)
Async XLA Ops:
  7.3 63.6 %all-gather.5.cloned.1.call-start = ((), (), s32[]{:S(2)}) async-start(), calls=%async_computation.6 | async-start | bytes 1843200 | tf_op jit(solution)/shard_map/all_gather | solution.py:1310
  7.3 12.0 %collective-permute-start.6 = (s32[2]{0:T(128)}, s32[2]{0:T(128)S(1)}, u32[]{:S(2)}, u32[]{:S(2)}) collective-permute-start(s32[2]{0:T(128)} %param.19), channel_id=1, source_target_pairs={{0,24},{8,0},{16,8},{24,16},{1,25},{9,1},{17,9},{25,17},{2,26},{10... | collective-permute-start | bytes 32 | tf_op jit(solution)/shard_map/ppermute | solution.py:488
  14.9 17.8 %collective-permute-start.13 = (bf16[48,1152]{1,0:T(8,128)(2,1)S(1)}, bf16[48,1152]{1,0:T(8,128)(2,1)S(1)}, u32[]{:S(2)}, u32[]{:S(2)}) collective-permute-start(bf16[48,1152]{1,0:T(8,128)(2,1)S(1)} %cut_attn.1), channel_id=1, source_target_pairs={{0,24},{8,0},{16,8},{24,16},{1,25},{9,1},{17,9},{25,17},{2,26},{10... | collective-permute-start | bytes 331784 | tf_op jit(solution)/shard_map/ppermute | solution.py:488
  17.8 15.0 %collective-permute-start.12 = (bf16[48,1152]{1,0:T(8,128)(2,1)S(1)}, bf16[48,1152]{1,0:T(8,128)(2,1)S(1)}, u32[]{:S(2)}, u32[]{:S(2)}) collective-permute-start(bf16[48,1152]{1,0:T(8,128)(2,1)S(1)} %cut_attn.1), channel_id=1, source_target_pairs={{0,16},{8,24},{16,0},{24,8},{1,17},{9,25},{17,1},{25,9},{2,18},{10... | collective-permute-start | bytes 331784 | tf_op jit(solution)/shard_map/ppermute | solution.py:488
  37.5 101.1 %all-gather.7.cloned.1.call-start = ((), (), s32[]{:S(2)}) async-start(), calls=%async_computation.7 | async-start | bytes 2764800 | tf_op jit(solution)/shard_map/all_gather | solution.py:1310
  55.0 368.2 %reduce-scatter.6.cloned.1.call-start = ((), (), s32[]{:S(2)}) async-start(), calls=%async_computation.4 | async-start | bytes 737280 | tf_op jit(solution)/shard_map/reduce_scatter | solution.py:1447
  73.3 25.5 %collective-permute-start.20 = (bf16[3,96,1920]{2,1,0:T(8,128)(2,1)S(1)}, bf16[3,96,1920]{2,1,0:T(8,128)(2,1)}, u32[]{:S(2)}, u32[]{:S(2)}) collective-permute-start(bf16[3,96,1920]{2,1,0:T(8,128)(2,1)S(1)} %others.2.refs_4_), channel_id=1, source_target_pairs={{0,4},{4,0},{1,5},{5,1},{2,6},{6,2},{3,7},{7,3},{8,12},{12,8},{9,1... | collective-permute-start | bytes 3317768 | tf_op jit(solution)/shard_map/ppermute | solution.py:476
  76.3 22.6 %collective-permute-start.19 = (bf16[3,96,1920]{2,1,0:T(8,128)(2,1)S(1)}, bf16[3,96,1920]{2,1,0:T(8,128)(2,1)}, u32[]{:S(2)}, u32[]{:S(2)}) collective-permute-start(bf16[3,96,1920]{2,1,0:T(8,128)(2,1)S(1)} %others.2.refs_4_), channel_id=1, source_target_pairs={{0,1},{1,0},{2,3},{3,2},{4,5},{5,4},{6,7},{7,6},{8,9},{9,8},{10,11... | collective-permute-start | bytes 3317768 | tf_op jit(solution)/shard_map/ppermute | solution.py:480
  111.6 11.3 %collective-permute-start.22 = (bf16[256,768]{1,0:T(8,128)(2,1)}, bf16[256,768]{1,0:T(8,128)(2,1)S(1)}, u32[]{:S(2)}, u32[]{:S(2)}) collective-permute-start(bf16[256,768]{1,0:T(8,128)(2,1)} %get-tuple-element.100.refs_0_), channel_id=1, source_target_pairs={{0,2},{2,0},{1,3},{3,1},{4,6},{6,4},{5,7},{7,5},{8,10},{10,8},{9,1... | collective-permute-start | bytes 1179656 | tf_op jit(solution)/shard_map/ppermute | solution.py:484
  151.5 27.1 %collective-permute-start.31 = (bf16[3,96,1920]{2,1,0:T(8,128)(2,1)}, bf16[3,96,1920]{2,1,0:T(8,128)(2,1)}, u32[]{:S(2)}, u32[]{:S(2)}) collective-permute-start(bf16[3,96,1920]{2,1,0:T(8,128)(2,1)} %get-tuple-element.111.refs_4_), channel_id=1, source_target_pairs={{0,4},{4,0},{1,5},{5,1},{2,6},{6,2},{3,7},{7,3},{8,12},{12,8},{9,1... | collective-permute-start | bytes 3317768 | tf_op jit(solution)/shard_map/ppermute | solution.py:476
  173.9 18.7 %collective-permute-start.30 = (bf16[3,96,1920]{2,1,0:T(8,128)(2,1)}, bf16[3,96,1920]{2,1,0:T(8,128)(2,1)}, u32[]{:S(2)}, u32[]{:S(2)}) collective-permute-start(bf16[3,96,1920]{2,1,0:T(8,128)(2,1)} %get-tuple-element.111.refs_4_), channel_id=1, source_target_pairs={{0,1},{1,0},{2,3},{3,2},{4,5},{5,4},{6,7},{7,6},{8,9},{9,8},{10,11... | collective-permute-start | bytes 3317768 | tf_op jit(solution)/shard_map/ppermute | solution.py:480
  178.8 13.8 %collective-permute-start.32 = (bf16[3,96,1920]{2,1,0:T(8,128)(2,1)}, bf16[3,96,1920]{2,1,0:T(8,128)(2,1)}, u32[]{:S(2)}, u32[]{:S(2)}) collective-permute-start(bf16[3,96,1920]{2,1,0:T(8,128)(2,1)} %hold.9.refs_6_), channel_id=1, source_target_pairs={{0,1},{1,0},{2,3},{3,2},{4,5},{5,4},{6,7},{7,6},{8,9},{9,8},{10,11... | collective-permute-start | bytes 3317768 | tf_op jit(solution)/shard_map/ppermute | solution.py:480
  191.1 10.9 %collective-permute-start.35 = (bf16[256,768]{1,0:T(8,128)(2,1)S(1)}, bf16[256,768]{1,0:T(8,128)(2,1)S(1)}, u32[]{:S(2)}, u32[]{:S(2)}) collective-permute-start(bf16[256,768]{1,0:T(8,128)(2,1)S(1)} %get-tuple-element.117.refs_0_.refs_1_), channel_id=1, source_target_pairs={{0,2},{2,0},{1,3},{3,1},{4,6},{6,4},{5,7},{7,5},{8,10},{10,8},{9,1... | collective-permute-start | bytes 1179656 | tf_op jit(solution)/shard_map/ppermute | solution.py:484
  219.4 30.9 %collective-permute-start.36 = (bf16[256,768]{1,0:T(8,128)(2,1)}, bf16[256,768]{1,0:T(8,128)(2,1)}, u32[]{:S(2)}, u32[]{:S(2)}) collective-permute-start(bf16[256,768]{1,0:T(8,128)(2,1)} %get-tuple-element.119), channel_id=1, source_target_pairs={{0,2},{2,0},{1,3},{3,1},{4,6},{6,4},{5,7},{7,5},{8,10},{10,8},{9,1... | collective-permute-start | bytes 1179656 | tf_op jit(solution)/shard_map/ppermute | solution.py:484
  229.6 14.7 %collective-permute-start.38 = (bf16[256,768]{1,0:T(8,128)(2,1)}, bf16[256,768]{1,0:T(8,128)(2,1)}, u32[]{:S(2)}, u32[]{:S(2)}) collective-permute-start(bf16[256,768]{1,0:T(8,128)(2,1)} %get-tuple-element.125), channel_id=1, source_target_pairs={{0,2},{2,0},{1,3},{3,1},{4,6},{6,4},{5,7},{7,5},{8,10},{10,8},{9,1... | collective-permute-start | bytes 1179656 | tf_op jit(solution)/shard_map/ppermute | solution.py:484
  238.9 36.8 %collective-permute-start.78 = (bf16[4,2,96,768]{3,2,0,1:T(8,128)(2,1)}, bf16[4,2,96,768]{3,2,0,1:T(8,128)(2,1)}, u32[]{:S(2)}, u32[]{:S(2)}) collective-permute-start(bf16[4,2,96,768]{3,2,0,1:T(8,128)(2,1)} %bitcast.245), channel_id=1, source_target_pairs={{0,1},{1,0},{2,3},{3,2},{4,5},{5,4},{6,7},{7,6},{8,9},{9,8},{10,11... | collective-permute-start | bytes 3538952 | tf_op jit(solution)/shard_map/ppermute | solution.py:480
  243.7 36.3 %collective-permute-start.76 = (bf16[4,2,48,1536]{3,2,0,1:T(8,128)(2,1)}, bf16[4,2,48,1536]{3,2,0,1:T(8,128)(2,1)}, u32[]{:S(2)}, u32[]{:S(2)}) collective-permute-start(bf16[4,2,48,1536]{3,2,0,1:T(8,128)(2,1)} %bitcast.246), channel_id=1, source_target_pairs={{0,1},{1,0},{2,3},{3,2},{4,5},{5,4},{6,7},{7,6},{8,9},{9,8},{10,11... | collective-permute-start | bytes 3538952 | tf_op jit(solution)/shard_map/ppermute | solution.py:480
  250.0 23.8 %collective-permute-start.73 = (bf16[4,2,48,768]{3,2,0,1:T(8,128)(2,1)}, bf16[4,2,48,768]{3,2,0,1:T(8,128)(2,1)}, u32[]{:S(2)}, u32[]{:S(2)}) collective-permute-start(bf16[4,2,48,768]{3,2,0,1:T(8,128)(2,1)} %bitcast.251), channel_id=1, source_target_pairs={{0,1},{1,0},{2,3},{3,2},{4,5},{5,4},{6,7},{7,6},{8,9},{9,8},{10,11... | collective-permute-start | bytes 1769480 | tf_op jit(solution)/shard_map/ppermute | solution.py:480
  252.3 219.0 %collective-permute-start.37 = (bf16[128,768]{1,0:T(8,128)(2,1)}, bf16[128,768]{1,0:T(8,128)(2,1)}, u32[]{:S(2)}, u32[]{:S(2)}) collective-permute-start(bf16[128,768]{1,0:T(8,128)(2,1)} %get-tuple-element.224), channel_id=1, source_target_pairs={{0,4},{4,0},{1,5},{5,1},{2,6},{6,2},{3,7},{7,3},{8,12},{12,8},{9,1... | collective-permute-start | bytes 589832 | tf_op jit(solution)/shard_map/ppermute | solution.py:476
  273.7 12.8 %collective-permute-start.40 = (bf16[512,768]{1,0:T(8,128)(2,1)S(1)}, bf16[512,768]{1,0:T(8,128)(2,1)S(1)}, u32[]{:S(2)}, u32[]{:S(2)}) collective-permute-start(bf16[512,768]{1,0:T(8,128)(2,1)S(1)} %get-tuple-element.132), channel_id=1, source_target_pairs={{0,1},{1,0},{2,3},{3,2},{4,5},{5,4},{6,7},{7,6},{8,9},{9,8},{10,11... | collective-permute-start | bytes 2359304 | tf_op jit(solution)/shard_map/ppermute | solution.py:480
  278.5 58.0 %collective-permute-start.79 = (bf16[4,96,768]{2,1,0:T(8,128)(2,1)}, bf16[4,96,768]{2,1,0:T(8,128)(2,1)}, u32[]{:S(2)}, u32[]{:S(2)}) collective-permute-start(bf16[4,96,768]{2,1,0:T(8,128)(2,1)} %dynamic-slice_bitcast_fusion), channel_id=1, source_target_pairs={{0,4},{4,0},{1,5},{5,1},{2,6},{6,2},{3,7},{7,3},{8,12},{12,8},{9,1... | collective-permute-start | bytes 1769480 | tf_op jit(solution)/shard_map/ppermute | solution.py:476
  282.5 53.9 %collective-permute-start.77 = (bf16[4,48,1536]{2,1,0:T(8,128)(2,1)}, bf16[4,48,1536]{2,1,0:T(8,128)(2,1)}, u32[]{:S(2)}, u32[]{:S(2)}) collective-permute-start(bf16[4,48,1536]{2,1,0:T(8,128)(2,1)} %dynamic-slice_bitcast_fusion.1), channel_id=1, source_target_pairs={{0,4},{4,0},{1,5},{5,1},{2,6},{6,2},{3,7},{7,3},{8,12},{12,8},{9,1... | collective-permute-start | bytes 1769480 | tf_op jit(solution)/shard_map/ppermute | solution.py:476
  285.1 20.7 %collective-permute-start.75 = (bf16[4,48,384]{2,1,0:T(8,128)(2,1)S(1)}, bf16[4,48,384]{2,1,0:T(8,128)(2,1)S(1)}, u32[]{:S(2)}, u32[]{:S(2)}) collective-permute-start(bf16[4,48,384]{2,1,0:T(8,128)(2,1)S(1)} %constant_dynamic-slice_fusion.4), channel_id=1, source_target_pairs={{0,2},{2,0},{1,3},{3,1},{4,6},{6,4},{5,7},{7,5},{8,10},{10,8},{9,1... | collective-permute-start | bytes 442376 | tf_op jit(solution)/shard_map/ppermute | solution.py:484
  304.9 32.1 %collective-permute-start.71 = (bf16[4,2,48,1152]{3,2,0,1:T(8,128)(2,1)}, bf16[4,2,48,1152]{3,2,0,1:T(8,128)(2,1)}, u32[]{:S(2)}, u32[]{:S(2)}) collective-permute-start(bf16[4,2,48,1152]{3,2,0,1:T(8,128)(2,1)} %bitcast.249), channel_id=1, source_target_pairs={{0,1},{1,0},{2,3},{3,2},{4,5},{5,4},{6,7},{7,6},{8,9},{9,8},{10,11... | collective-permute-start | bytes 2654216 | tf_op jit(solution)/shard_map/ppermute | solution.py:480
  305.8 11.6 %collective-permute-start.42 = (bf16[256,768]{1,0:T(8,128)(2,1)S(1)}, bf16[256,768]{1,0:T(8,128)(2,1)S(1)}, u32[]{:S(2)}, u32[]{:S(2)}) collective-permute-start(bf16[256,768]{1,0:T(8,128)(2,1)S(1)} %get-tuple-element.137.refs_0_), channel_id=1, source_target_pairs={{0,2},{2,0},{1,3},{3,1},{4,6},{6,4},{5,7},{7,5},{8,10},{10,8},{9,1... | collective-permute-start | bytes 1179656 | tf_op jit(solution)/shard_map/ppermute | solution.py:484
  327.9 13.2 %collective-permute-start.43 = (bf16[256,768]{1,0:T(8,128)(2,1)}, bf16[256,768]{1,0:T(8,128)(2,1)S(1)}, u32[]{:S(2)}, u32[]{:S(2)}) collective-permute-start(bf16[256,768]{1,0:T(8,128)(2,1)} %get-tuple-element.140), channel_id=1, source_target_pairs={{0,2},{2,0},{1,3},{3,1},{4,6},{6,4},{5,7},{7,5},{8,10},{10,8},{9,1... | collective-permute-start | bytes 1179656 | tf_op jit(solution)/shard_map/ppermute | solution.py:484
  336.5 35.1 %collective-permute-start.64 = (bf16[4,2,96,768]{3,2,0,1:T(8,128)(2,1)}, bf16[4,2,96,768]{3,2,0,1:T(8,128)(2,1)}, u32[]{:S(2)}, u32[]{:S(2)}) collective-permute-start(bf16[4,2,96,768]{3,2,0,1:T(8,128)(2,1)} %bitcast.247), channel_id=1, source_target_pairs={{0,1},{1,0},{2,3},{3,2},{4,5},{5,4},{6,7},{7,6},{8,9},{9,8},{10,11... | collective-permute-start | bytes 3538952 | tf_op jit(solution)/shard_map/ppermute | solution.py:480
  336.5 38.9 %collective-permute-start.62 = (bf16[4,2,48,1536]{3,2,0,1:T(8,128)(2,1)}, bf16[4,2,48,1536]{3,2,0,1:T(8,128)(2,1)}, u32[]{:S(2)}, u32[]{:S(2)}) collective-permute-start(bf16[4,2,48,1536]{3,2,0,1:T(8,128)(2,1)} %bitcast.306), channel_id=1, source_target_pairs={{0,1},{1,0},{2,3},{3,2},{4,5},{5,4},{6,7},{7,6},{8,9},{9,8},{10,11... | collective-permute-start | bytes 3538952 | tf_op jit(solution)/shard_map/ppermute | solution.py:480
  338.9 21.1 %collective-permute-start.72 = (bf16[4,48,1152]{2,1,0:T(8,128)(2,1)S(1)}, bf16[4,48,1152]{2,1,0:T(8,128)(2,1)S(1)}, u32[]{:S(2)}, u32[]{:S(2)}) collective-permute-start(bf16[4,48,1152]{2,1,0:T(8,128)(2,1)S(1)} %dynamic-slice_bitcast_fusion.4), channel_id=1, source_target_pairs={{0,4},{4,0},{1,5},{5,1},{2,6},{6,2},{3,7},{7,3},{8,12},{12,8},{9,1... | collective-permute-start | bytes 1327112 | tf_op jit(solution)/shard_map/ppermute | solution.py:476
  363.9 59.2 %reduce-scatter.8.cloned.1.call-start = ((), (), s32[]{:S(2)}) async-start(), calls=%async_computation.5 | async-start | bytes 1474560 | tf_op jit(solution)/shard_map/reduce_scatter | solution.py:1447
  368.2 89.6 %reduce-scatter.4.cloned.1.call-start = ((), (), s32[]{:S(2)}) async-start(), calls=%async_computation.3 | async-start | bytes 1474560 | tf_op jit(solution)/shard_map/reduce_scatter | solution.py:1447
  368.4 13.5 %collective-permute-start.45 = (bf16[512,768]{1,0:T(8,128)(2,1)}, bf16[512,768]{1,0:T(8,128)(2,1)S(1)}, u32[]{:S(2)}, u32[]{:S(2)}) collective-permute-start(bf16[512,768]{1,0:T(8,128)(2,1)} %copy-done.111), channel_id=1, source_target_pairs={{0,1},{1,0},{2,3},{3,2},{4,5},{5,4},{6,7},{7,6},{8,9},{9,8},{10,11... | collective-permute-start | bytes 2359304 | tf_op jit(solution)/shard_map/ppermute | solution.py:480
  374.4 28.6 %collective-permute-start.65 = (bf16[4,96,768]{2,1,0:T(8,128)(2,1)}, bf16[4,96,768]{2,1,0:T(8,128)(2,1)S(1)}, u32[]{:S(2)}, u32[]{:S(2)}) collective-permute-start(bf16[4,96,768]{2,1,0:T(8,128)(2,1)} %dynamic-slice_bitcast_fusion.2), channel_id=1, source_target_pairs={{0,4},{4,0},{1,5},{5,1},{2,6},{6,2},{3,7},{7,3},{8,12},{12,8},{9,1... | collective-permute-start | bytes 1769480 | tf_op jit(solution)/shard_map/ppermute | solution.py:476
  377.9 27.1 %collective-permute-start.63 = (bf16[4,48,1536]{2,1,0:T(8,128)(2,1)}, bf16[4,48,1536]{2,1,0:T(8,128)(2,1)}, u32[]{:S(2)}, u32[]{:S(2)}) collective-permute-start(bf16[4,48,1536]{2,1,0:T(8,128)(2,1)} %dynamic-slice_bitcast_fusion.3), channel_id=1, source_target_pairs={{0,4},{4,0},{1,5},{5,1},{2,6},{6,2},{3,7},{7,3},{8,12},{12,8},{9,1... | collective-permute-start | bytes 1769480 | tf_op jit(solution)/shard_map/ppermute | solution.py:476
  380.6 13.2 %collective-permute-start.58 = (bf16[4,48,384]{2,1,0:T(8,128)(2,1)S(1)}, bf16[4,48,384]{2,1,0:T(8,128)(2,1)S(1)}, u32[]{:S(2)}, u32[]{:S(2)}) collective-permute-start(bf16[4,48,384]{2,1,0:T(8,128)(2,1)S(1)} %constant_dynamic-slice_fusion.13), channel_id=1, source_target_pairs={{0,2},{2,0},{1,3},{3,1},{4,6},{6,4},{5,7},{7,5},{8,10},{10,8},{9,1... | collective-permute-start | bytes 442376 | tf_op jit(solution)/shard_map/ppermute | solution.py:484
  393.8 15.2 %collective-permute-start.54 = (bf16[4,2,48,1152]{3,2,0,1:T(8,128)(2,1)}, bf16[4,2,48,1152]{3,2,0,1:T(8,128)(2,1)}, u32[]{:S(2)}, u32[]{:S(2)}) collective-permute-start(bf16[4,2,48,1152]{3,2,0,1:T(8,128)(2,1)} %bitcast.250), channel_id=1, source_target_pairs={{0,1},{1,0},{2,3},{3,2},{4,5},{5,4},{6,7},{7,6},{8,9},{9,8},{10,11... | collective-permute-start | bytes 2654216 | tf_op jit(solution)/shard_map/ppermute | solution.py:480
  410.4 11.2 %collective-permute-start.55 = (bf16[4,48,1152]{2,1,0:T(8,128)(2,1)S(1)}, bf16[4,48,1152]{2,1,0:T(8,128)(2,1)S(1)}, u32[]{:S(2)}, u32[]{:S(2)}) collective-permute-start(bf16[4,48,1152]{2,1,0:T(8,128)(2,1)S(1)} %dynamic-slice_bitcast_fusion.5), channel_id=1, source_target_pairs={{0,4},{4,0},{1,5},{5,1},{2,6},{6,2},{3,7},{7,3},{8,12},{12,8},{9,1... | collective-permute-start | bytes 1327112 | tf_op jit(solution)/shard_map/ppermute | solution.py:476
  412.4 21.6 %collective-permute-start.49 = (f32[2,4,2496]{2,1,0:T(4,128)S(1)}, f32[2,4,2496]{2,1,0:T(4,128)S(1)}, u32[]{:S(2)}, u32[]{:S(2)}) collective-permute-start(f32[2,4,2496]{2,1,0:T(4,128)S(1)} %fusion.62), channel_id=1, source_target_pairs={{0,1},{1,0},{2,3},{3,2},{4,5},{5,4},{6,7},{7,6},{8,9},{9,8},{10,11... | collective-permute-start | bytes 239624 | tf_op jit(solution)/shard_map/ppermute | solution.py:480
  435.0 14.1 %collective-permute-start.61 = (bf16[48,1536]{1,0:T(8,128)(2,1)S(1)}, bf16[48,1536]{1,0:T(8,128)(2,1)S(1)}, u32[]{:S(2)}, u32[]{:S(2)}) collective-permute-start(bf16[48,1536]{1,0:T(8,128)(2,1)S(1)} %get-tuple-element.216), channel_id=1, source_target_pairs={{0,24},{8,0},{16,8},{24,16},{1,25},{9,1},{17,9},{25,17},{2,26},{10... | collective-permute-start | bytes 442376 | tf_op jit(solution)/shard_map/ppermute | solution.py:488
  438.6 17.6 %collective-permute-start.60 = (bf16[48,1536]{1,0:T(8,128)(2,1)S(1)}, bf16[48,1536]{1,0:T(8,128)(2,1)S(1)}, u32[]{:S(2)}, u32[]{:S(2)}) collective-permute-start(bf16[48,1536]{1,0:T(8,128)(2,1)S(1)} %get-tuple-element.215), channel_id=1, source_target_pairs={{0,16},{8,24},{16,0},{24,8},{1,17},{9,25},{17,1},{25,9},{2,18},{10... | collective-permute-start | bytes 442376 | tf_op jit(solution)/shard_map/ppermute | solution.py:488
  440.0 35.2 %collective-permute-start.52 = (f32[2,2496]{1,0:T(2,128)S(1)}, f32[2,2496]{1,0:T(2,128)S(1)}, u32[]{:S(2)}, u32[]{:S(2)}) collective-permute-start(f32[2,2496]{1,0:T(2,128)S(1)} %bitcast.333), channel_id=1, source_target_pairs={{0,24},{8,0},{16,8},{24,16},{1,25},{9,1},{17,9},{25,17},{2,26},{10... | collective-permute-start | bytes 59912 | tf_op jit(solution)/shard_map/ppermute | solution.py:488
  441.5 14.8 %collective-permute-start.81 = (bf16[144,1536]{1,0:T(8,128)(2,1)}, bf16[144,1536]{1,0:T(8,128)(2,1)S(1)}, u32[]{:S(2)}, u32[]{:S(2)}) collective-permute-start(bf16[144,1536]{1,0:T(8,128)(2,1)} %hold.15), channel_id=1, source_target_pairs={{0,2},{2,0},{1,3},{3,1},{4,6},{6,4},{5,7},{7,5},{8,10},{10,8},{9,1... | collective-permute-start | bytes 1327112 | tf_op jit(solution)/shard_map/ppermute | solution.py:484
  449.0 16.6 %collective-permute-start.83 = (bf16[80,1536]{1,0:T(8,128)(2,1)S(1)}, bf16[80,1536]{1,0:T(8,128)(2,1)S(1)}, u32[]{:S(2)}, u32[]{:S(2)}) collective-permute-start(bf16[80,1536]{1,0:T(8,128)(2,1)S(1)} %slice.265), channel_id=1, source_target_pairs={{0,2},{2,0},{1,3},{3,1},{4,6},{6,4},{5,7},{7,5},{8,10},{10,8},{9,1... | collective-permute-start | bytes 737288 | tf_op jit(solution)/shard_map/ppermute | solution.py:484
  458.8 10.6 %collective-permute-start.66 = (bf16[144,1536]{1,0:T(8,128)(2,1)S(1)}, bf16[144,1536]{1,0:T(8,128)(2,1)S(1)}, u32[]{:S(2)}, u32[]{:S(2)}) collective-permute-start(bf16[144,1536]{1,0:T(8,128)(2,1)S(1)} %get-tuple-element.219), channel_id=1, source_target_pairs={{0,4},{4,0},{1,5},{5,1},{2,6},{6,2},{3,7},{7,3},{8,12},{12,8},{9,1... | collective-permute-start | bytes 1327112 | tf_op jit(solution)/shard_map/ppermute | solution.py:476
  464.2 10.9 %collective-permute-start.67 = (bf16[144,1536]{1,0:T(8,128)(2,1)S(1)}, bf16[144,1536]{1,0:T(8,128)(2,1)S(1)}, u32[]{:S(2)}, u32[]{:S(2)}) collective-permute-start(bf16[144,1536]{1,0:T(8,128)(2,1)S(1)} %get-tuple-element.219), channel_id=1, source_target_pairs={{0,2},{2,0},{1,3},{3,1},{4,6},{6,4},{5,7},{7,5},{8,10},{10,8},{9,1... | collective-permute-start | bytes 1327112 | tf_op jit(solution)/shard_map/ppermute | solution.py:484
  465.9 26.8 %collective-permute-start.84 = (bf16[4,144,1536]{2,1,0:T(8,128)(2,1)S(1)}, bf16[4,144,1536]{2,1,0:T(8,128)(2,1)S(1)}, u32[]{:S(2)}, u32[]{:S(2)}) collective-permute-start(bf16[4,144,1536]{2,1,0:T(8,128)(2,1)S(1)} %fusion.9), channel_id=1, source_target_pairs={{0,1},{1,0},{2,3},{3,2},{4,5},{5,4},{6,7},{7,6},{8,9},{9,8},{10,11... | collective-permute-start | bytes 5308424 | tf_op jit(solution)/shard_map/ppermute | solution.py:480
  469.5 12.8 %collective-permute-start.69 = (bf16[80,1536]{1,0:T(8,128)(2,1)S(1)}, bf16[80,1536]{1,0:T(8,128)(2,1)S(1)}, u32[]{:S(2)}, u32[]{:S(2)}) collective-permute-start(bf16[80,1536]{1,0:T(8,128)(2,1)S(1)} %slice.256), channel_id=1, source_target_pairs={{0,2},{2,0},{1,3},{3,1},{4,6},{6,4},{5,7},{7,5},{8,10},{10,8},{9,1... | collective-permute-start | bytes 737288 | tf_op jit(solution)/shard_map/ppermute | solution.py:484
  482.6 14.5 %collective-permute-start.70 = (bf16[4,144,1536]{2,1,0:T(8,128)(2,1)S(1)}, bf16[4,144,1536]{2,1,0:T(8,128)(2,1)S(1)}, u32[]{:S(2)}, u32[]{:S(2)}) collective-permute-start(bf16[4,144,1536]{2,1,0:T(8,128)(2,1)S(1)} %fusion.13), channel_id=1, source_target_pairs={{0,1},{1,0},{2,3},{3,2},{4,5},{5,4},{6,7},{7,6},{8,9},{9,8},{10,11... | collective-permute-start | bytes 5308424 | tf_op jit(solution)/shard_map/ppermute | solution.py:480
  (205 other events, 1209.9 us)
Sparse Core Ops, SparseCore 0:
  37.6 33.1 all-gather.4
  73.0 46.9 all-gather.6
  364.0 21.1 reduce-scatter.5
  387.9 27.5 reduce-scatter.7
  418.3 36.1 reduce-scatter.3
where the time goes:
time: 514 us; the launch traced here: 508 us
  waiting for transfers between devices  154 us (30%)
  Pallas kernels  123 us (24%)
  local copies, waits for them, and re-layouts  82.4 us (16%)
  starting transfers between devices  79.9 us (16%)
  other arithmetic  38.5 us (7%)
  between operations  16.6 us (3%)
  matrix products  14.2 us (3%)
    ppermute x22, waiting for transfers between devices, swap_blk(): return lax.ppermute(value, 'blk', SWAP)  59.5 us
    ppermute x24, waiting for transfers between devices, swap_core(): return lax.ppermute(value, 'uly', ACROSS)  55.7 us
    unnamed x337, local copies, waits for them, and re-layouts  45.5 us
    pallas_call x4, Pallas kernels, chunk_call(): pl.pallas_call(lambda *refs: kernel(*refs[:first_out], *refs[first_out +...  29.1 us
    ppermute x15, waiting for transfers between devices, from_shard(): lax.ppermute(value, 'dp', [(at, (at + back) % shards) for at in range(sha...  28.4 us
    pallas_call x4, Pallas kernels, attend_back(): pl.pallas_call(lambda *refs: back_kernel(more is not None, *refs[:first_o...  28.3 us
    ppermute x24, starting transfers between devices, swap_core(): return lax.ppermute(value, 'uly', ACROSS)  27.8 us
    ppermute x22, starting transfers between devices, swap_blk(): return lax.ppermute(value, 'blk', SWAP)  26.3 us
  transfers between devices with their start and end apart: 90, of which 42 were waited for; matrix products, arithmetic and copies ran while one was open for 18% of the time, Pallas kernels for 22%

commit v1 on v0

--- a/solution.py
+++ b/solution.py
@@ -1391,7 +1391,7 @@
         att_own, att_send, lse = attend(query, near, far, seg_q, seg_k, ())
         att_other = swap_core(att_send)
         if index == 0:
-            mlp_own = others(place, mlp_whole, [(0, 2 * rows_in, mlp_columns)], [att_own])[0]
+            mlp_own = others(place, mlp_whole, [(0, 2 * rows_in, mlp_columns)], [query])[0]
         mlp = spread_late(mlp_own, att_other)
         out_whole, hiddens, downs = whole_mlp(index, mlp)
         gathered.append((hiddens, downs))
@@ -1458,7 +1458,10 @@
     )[0]
     def end_mlp_sums(pending, late):
         index, down_pair, hidden_pair, _, _ = pending
-        down_sum, hidden_sum = reduce_end(down_pair, late), reduce_end(hidden_pair, late)
+        down_sum, hidden_sum = (
+            reduce_end(down_pair, *((late,) if pending[0] == 0 else ())),
+            reduce_end(hidden_pair, *((late,) if pending[0] == 0 else ())),
+        )
         down_sum = jnp.concatenate([down_sum[:, :rows_in], down_sum[:, rows_in:]], axis=2)
         return scatter_shards(jnp.concatenate([hidden_sum, down_sum], axis=1))
 
@@ -1550,11 +1553,12 @@
         )
         sums_top = sums_next
 
+    attn_arrived = pending[3][1]
     attn_shard, shard_arrived = end_attn_sums(pending, None)
     shards_out[0] = (attn_shard, end_mlp_sums(pending, last_grad))
     tokens_grad = give_back(last_grad)
 
-    vector = jnp.stack(small)
+    vector = hold(jnp.stack(small), token(attn_arrived))
     vector = vector + swap_core(vector)
     vector = vector + swap_half(vector)
     parts = vector.transpose(1, 0, 2)
@@ -1597,7 +1601,7 @@
     for index in reversed(range(layers)):
         piece = jnp.concatenate(shards_out[index], axis=0)
         if index > 0:
-            piece = hold(piece, token(shard_arrived))
+            pass
         grads = finish(
             place, index, ("attn", "mlp"), every_piece(piece, None), shapes, half, rows_in, shards, grads
         )

time: 514 us -> 493 us (0.959)
  local copies, waits for them, and re-layouts: 82.4 us -> 63.6 us
    ppermute x22, waiting for transfers between devices: 59.5 us -> 42.6 us  [swap_blk(): return lax.ppermute(value, 'blk', SWAP)]
    ppermute x24, waiting for transfers between devices: 55.7 us -> 70.4 us  [swap_core(): return lax.ppermute(value, 'uly', ACROSS)]
    unnamed x337 -> x255, local copies, waits for them, and re-layouts: 45.5 us -> 31.7 us
    ppermute x15, waiting for transfers between devices: 28.4 us -> 21.1 us  [from_shard(): lax.ppermute(value, 'dp', [(at, (at + back) % shards) for at in range(sha...]
    all_gather x2, waiting for transfers between devices: 3.29 us -> 8.98 us  [every_shard_of(): return lax.all_gather(piece, 'dp', axis=0, tiled=False)]
  transfers between devices with their start and end apart: 90 -> 90, of which waited for: 42 -> 44; matrix products, arithmetic and copies ran while one was open for 18% -> 17% of each run, Pallas kernels for 22% -> 23%
where the time goes in v1:
time: 493 us; the launch traced here: 488 us
  waiting for transfers between devices  154 us (31%)
  Pallas kernels  122 us (25%)
  starting transfers between devices  80.9 us (16%)
  local copies, waits for them, and re-layouts  63.6 us (13%)
  other arithmetic  37.9 us (8%)
  between operations  16.2 us (3%)
  matrix products  14.3 us (3%)
    ppermute x24, waiting for transfers between devices, swap_core(): return lax.ppermute(value, 'uly', ACROSS)  70.4 us
    ppermute x22, waiting for transfers between devices, swap_blk(): return lax.ppermute(value, 'blk', SWAP)  42.6 us
    unnamed x255, local copies, waits for them, and re-layouts  31.7 us
    ppermute x24, starting transfers between devices, swap_core(): return lax.ppermute(value, 'uly', ACROSS)  31.6 us
    pallas_call x4, Pallas kernels, attend_back(): pl.pallas_call(lambda *refs: back_kernel(more is not None, *refs[:first_o...  28.4 us
    pallas_call x4, Pallas kernels, chunk_call(): pl.pallas_call(lambda *refs: kernel(*refs[:first_out], *refs[first_out +...  27.9 us
    ppermute x22, starting transfers between devices, swap_blk(): return lax.ppermute(value, 'blk', SWAP)  26.6 us
    pallas_call x9, Pallas kernels, copy_call(): pl.pallas_call(kernel, out_shape=tuple((pltpu.VMEM(shape, kind) if keep e...  22.8 us
  transfers between devices with their start and end apart: 90, of which 44 were waited for; matrix products, arithmetic and copies ran while one was open for 17% of the time, Pallas kernels for 23%

profile of v1, /device:TPU:0, one launch (start us, length us, event | category | flops | bytes accessed | tf_op | source)
XLA Modules:
  0.0 488.4 jit_solution(16231690164384434295)
XLA Ops:
  7.3 5.1 %collective-permute-start.6 = (s32[2]{0:T(128)}, s32[2]{0:T(128)S(1)}, u32[]{:S(2)}, u32[]{:S(2)}) collective-permute-start(s32[2]{0:T(128)} %param.19), channel_id=1, source_target_pairs={{0,24},{8,0},{16,8},{24,16},{1,25},{9,1},{17,9},{25,17},{2,26},{10... | collective-permute-start | bytes 32 | tf_op jit(solution)/shard_map/ppermute | solution.py:488
  14.9 2.9 collective-permute-start.13
  22.7 5.2 %collective-permute-done.12 = bf16[48,1152]{1,0:T(8,128)(2,1)S(1)} collective-permute-done((bf16[48,1152]{1,0:T(8,128)(2,1)S(1)}, bf16[48,1152]{1,0:T(8,128)(2,1)S(1)}, u32[]{:S(2)}, u32[]{:S(2)}) %collective-permute-start.12) | collective-permute-done | bytes 110624 | tf_op jit(solution)/shard_map/ppermute | solution.py:488
  28.0 2.4 cut_mlp.1.refs_5_
  41.1 2.5 cut_next.1
  48.5 2.6 join_attn.2
  51.2 2.8 collective-permute-done.10.refs_1_
  56.2 9.0 %all-gather.5.cloned.1.call-done = bf16[384,1920]{1,0:T(8,128)(2,1)} async-done(((bf16[96,1920]{1,0:T(8,128)(2,1)}), bf16[384,1920]{1,0:T(8,128)(2,1)}) %all-gather.5.cloned.1.call-update) | async-done | bytes 1474576 | tf_op jit(solution)/shard_map/all_gather | solution.py:1310
  72.6 9.0 %attend.2 = (bf16[256,384]{1,0:T(8,128)(2,1)S(1)}, bf16[256,384]{1,0:T(8,128)(2,1)S(1)}, f32[512,384]{1,0:T(8,128)}) custom-call(s32[512,1]{1,0:T(8,128)S(1)} %copy.46.seg_q_ref.refs_0_, s32[1,1024]{1,0:T(1,128)S(1)} %pad_add_fusion.seg_k_ref, bf16[512,384]{1,0:T(8,128)(2,1)S(1)} %queries.2.q_ref.refs_2_, ...), custom_call_target="tpu_custom_call" | custom-call | tf_op jit(solution)/shard_map/attend/pallas_call | solution.py:1088
  84.5 4.8 collective-permute-done.18.refs_1_.refs_2_
  89.2 5.1 %collective-permute-done.20.refs_0_ = bf16[3,96,1920]{2,1,0:T(8,128)(2,1)} collective-permute-done((bf16[3,96,1920]{2,1,0:T(8,128)(2,1)}, bf16[3,96,1920]{2,1,0:T(8,128)(2,1)}, u32[]{:S(2)}, u32[]{:S(2)}) %collective-permute-start.20) | collective-permute-done | bytes 1105952 | tf_op jit(solution)/shard_map/ppermute | solution.py:476
  94.5 2.9 collective-permute-done.21.refs_7_
  97.4 3.6 join_mlp.2
  109.0 9.8 %collective-permute-done.22.refs_1_ = bf16[256,768]{1,0:T(8,128)(2,1)S(1)} collective-permute-done((bf16[256,768]{1,0:T(8,128)(2,1)}, bf16[256,768]{1,0:T(8,128)(2,1)S(1)}, u32[]{:S(2)}, u32[]{:S(2)}) %collective-permute-start.22) | collective-permute-done | bytes 393248 | tf_op jit(solution)/shard_map/ppermute | solution.py:484
  123.9 8.1 %mlp.2 = (bf16[512,1536]{1,0:T(8,128)(2,1)}, bf16[512,1536]{1,0:T(8,128)(2,1)}, f32[256,768]{1,0:T(8,128)S(1)}, bf16[256,768]{1,0:T(8,128)(2,1)}, bf16[512,768]{1,0:T(8,128)(2,1)S(1)}) custom-call(bf16[256,768]{1,0:T(8,128)(2,1)} %get-tuple-element.100.refs_0_, bf16[256,768]{1,0:T(8,128)(2,1)S(1)} %copy-done.69, bf16[768,1536]{1,0:T(8,128)(2,1)S(1)} %bitcast.279, ...), custom_call_target="tpu_custom_call" | custom-call | tf_op jit(solution)/shard_map/mlp/pallas_call | solution.py:846
  140.2 3.3 collective-permute-done.23.refs_1_
  151.8 3.4 collective-permute-done.24.refs_1_
  159.2 8.5 %attend.3 = (bf16[256,384]{1,0:T(8,128)(2,1)S(1)}, bf16[256,384]{1,0:T(8,128)(2,1)S(1)}, f32[512,384]{1,0:T(8,128)}) custom-call(s32[512,1]{1,0:T(8,128)S(1)} %copy-done.5, s32[1,1024]{1,0:T(1,128)S(1)} %pad_add_fusion.seg_k_ref, bf16[512,384]{1,0:T(8,128)(2,1)S(1)} %queries.3.q_ref.refs_2_, ...), custom_call_target="tpu_custom_call" | custom-call | tf_op jit(solution)/shard_map/attend/pallas_call | solution.py:1088
  170.5 4.0 collective-permute-done.31.refs_0_
  181.0 4.6 collective-permute-done.34
  189.1 3.9 join_mlp.3
  196.9 2.8 collective-permute-done.35.refs_5_.refs_1_
  199.7 7.2 %collective-permute-done.33.refs_1_ = bf16[256,768]{1,0:T(8,128)(2,1)S(1)} collective-permute-done((bf16[256,768]{1,0:T(8,128)(2,1)S(1)}, bf16[256,768]{1,0:T(8,128)(2,1)S(1)}, u32[]{:S(2)}, u32[]{:S(2)}) %collective-permute-start.33) | collective-permute-done | bytes 393248 | tf_op jit(solution)/shard_map/ppermute | solution.py:484
  206.8 7.1 %mlp.3 = (bf16[512,1536]{1,0:T(8,128)(2,1)}, bf16[512,1536]{1,0:T(8,128)(2,1)}, f32[256,768]{1,0:T(8,128)S(1)}, bf16[256,768]{1,0:T(8,128)(2,1)S(1)}, bf16[512,768]{1,0:T(8,128)(2,1)S(1)}) custom-call(bf16[256,768]{1,0:T(8,128)(2,1)S(1)} %get-tuple-element.114.refs_0_, bf16[256,768]{1,0:T(8,128)(2,1)S(1)} %collective-permute-done.33.refs_1_, ...), custom_call_target="tpu_custom_call" | custom-call | tf_op jit(solution)/shard_map/mlp/pallas_call | solution.py:846
  215.4 6.6 %mlp_back.2 = (bf16[512,1536]{1,0:T(8,128)(2,1)S(1)}, f32[256,768]{1,0:T(8,128)S(1)}, bf16[256,768]{1,0:T(8,128)(2,1)S(1)}, f32[1,1536]{1,0:T(1,128)S(1)}, bf16[512,768]{1,0:T(8,128)(2,1)S(1)}) custom-call(bf16[256,768]{1,0:T(8,128)(2,1)S(1)} %get-tuple-element.117.refs_0_.refs_1_, bf16[256,768]{1,0:T(8,128)(2,1)S(1)} %collective-permute-done.35.refs_5_.refs_1_, ...), custom_call_target="tpu_custom_call" | custom-call | tf_op jit(solution)/shard_map/mlp_back/pallas_call | solution.py:846
  232.2 2.5 middle_back.2
  252.8 6.9 %attend_back.4 = (f32[512,384]{1,0:T(8,128)S(1)}, bf16[512,768]{1,0:T(8,128)(2,1)S(1)}) custom-call(s32[512,1]{1,0:T(8,128)S(1)} %copy-done.6, s32[1,512]{1,0:T(1,128)S(1)} %bitcast.294, bf16[512,384]{1,0:T(8,128)(2,1)S(1)} %copy-done.22, bf16[512,768]{1,0:T(8,128)(2,1)S(1)} %copy-done.10, bf16[512,768]{1,0:T(8,128)(2,1)S(1)} %copy-done.10, ...), custom_call_target="tpu_custom_call" | custom-call | tf_op jit(solution)/shard_map/attend_back/pallas_call | solution.py:1201
  266.0 7.3 %attend_back.5.refs_0_ = bf16[512,1152]{1,0:T(8,128)(2,1)S(1)} custom-call(s32[512,1]{1,0:T(8,128)S(1)} %copy-done.7, s32[1,512]{1,0:T(1,128)S(1)} %bitcast.291, bf16[512,384]{1,0:T(8,128)(2,1)S(1)} %copy-done.23, bf16[512,768]{1,0:T(8,128)(2,1)S(1)} %copy-done.3, bf16[512,768]{1,0:T(8,128)(2,1)S(1)} %copy-done.3, bf16[256,384]{1,0:T(8,128)(2,1)S(1)} %copy-done.57, ...), custom_call_target="tpu_custom_call" | custom-call | tf_op jit(solution)/shard_map/attend_back/pallas_call | solution.py:1201
  277.6 8.0 %collective-permute-done.41.refs_2_ = bf16[256,768]{1,0:T(8,128)(2,1)S(1)} collective-permute-done((bf16[256,768]{1,0:T(8,128)(2,1)S(1)}, bf16[256,768]{1,0:T(8,128)(2,1)S(1)}, u32[]{:S(2)}, u32[]{:S(2)}) %collective-permute-start.41) | collective-permute-done | bytes 393248 | tf_op jit(solution)/shard_map/ppermute | solution.py:484
  290.4 8.0 %collective-permute-done.42.refs_1_ = bf16[256,768]{1,0:T(8,128)(2,1)S(1)} collective-permute-done((bf16[256,768]{1,0:T(8,128)(2,1)S(1)}, bf16[256,768]{1,0:T(8,128)(2,1)S(1)}, u32[]{:S(2)}, u32[]{:S(2)}) %collective-permute-start.42) | collective-permute-done | bytes 393248 | tf_op jit(solution)/shard_map/ppermute | solution.py:484
  298.4 6.1 %mlp_back.3 = (bf16[512,1536]{1,0:T(8,128)(2,1)S(1)}, f32[256,768]{1,0:T(8,128)S(1)}, bf16[256,768]{1,0:T(8,128)(2,1)S(1)}, f32[1,1536]{1,0:T(1,128)S(1)}, bf16[512,768]{1,0:T(8,128)(2,1)S(1)}) custom-call(bf16[256,768]{1,0:T(8,128)(2,1)S(1)} %get-tuple-element.137.refs_0_, bf16[256,768]{1,0:T(8,128)(2,1)S(1)} %collective-permute-done.42.refs_1_, ...), custom_call_target="tpu_custom_call" | custom-call | tf_op jit(solution)/shard_map/mlp_back/pallas_call | solution.py:846
  307.8 7.1 %collective-permute-done.43.refs_3_ = bf16[256,768]{1,0:T(8,128)(2,1)S(1)} collective-permute-done((bf16[256,768]{1,0:T(8,128)(2,1)S(1)}, bf16[256,768]{1,0:T(8,128)(2,1)S(1)}, u32[]{:S(2)}, u32[]{:S(2)}) %collective-permute-start.43) | collective-permute-done | bytes 393248 | tf_op jit(solution)/shard_map/ppermute | solution.py:484
  315.5 2.5 middle_back.3
  320.2 3.5 collective-permute-done.44.refs_6_
  323.7 6.9 %attend_back.6 = (f32[512,384]{1,0:T(8,128)S(1)}, bf16[512,768]{1,0:T(8,128)(2,1)S(1)}) custom-call(s32[512,1]{1,0:T(8,128)S(1)} %copy-done.7, s32[1,512]{1,0:T(1,128)S(1)} %bitcast.295, bf16[512,384]{1,0:T(8,128)(2,1)S(1)} %copy-done.12, bf16[512,768]{1,0:T(8,128)(2,1)} %collective-permute-done.17.kf_ref.vf_ref.refs_3_.refs_4_, ...), custom_call_target="tpu_custom_call" | custom-call | tf_op jit(solution)/shard_map/attend_back/pallas_call | solution.py:1201
  340.8 3.1 convolution_convert_fusion.3
  368.5 7.4 %attend_back.7.refs_0_ = bf16[512,1152]{1,0:T(8,128)(2,1)S(1)} custom-call(s32[512,1]{1,0:T(8,128)S(1)} %copy-done.8, s32[1,512]{1,0:T(1,128)S(1)} %bitcast.292, bf16[512,384]{1,0:T(8,128)(2,1)S(1)} %copy-done.12, bf16[512,768]{1,0:T(8,128)(2,1)S(1)} %copy-done.1, bf16[512,768]{1,0:T(8,128)(2,1)S(1)} %copy-done.1, ...), custom_call_target="tpu_custom_call" | custom-call | tf_op jit(solution)/shard_map/attend_back/pallas_call | solution.py:1201
  380.3 6.7 %collective-permute-done.46.refs_2_ = bf16[256,768]{1,0:T(8,128)(2,1)S(1)} collective-permute-done((bf16[256,768]{1,0:T(8,128)(2,1)S(1)}, bf16[256,768]{1,0:T(8,128)(2,1)S(1)}, u32[]{:S(2)}, u32[]{:S(2)}) %collective-permute-start.46) | collective-permute-done | bytes 393248 | tf_op jit(solution)/shard_map/ppermute | solution.py:484
  388.4 3.3 collective-permute-done.63.refs_0_
  404.0 6.8 %collective-permute-done.80 = bf16[144,1536]{1,0:T(8,128)(2,1)S(1)} collective-permute-done((bf16[144,1536]{1,0:T(8,128)(2,1)}, bf16[144,1536]{1,0:T(8,128)(2,1)S(1)}, u32[]{:S(2)}, u32[]{:S(2)}) %collective-permute-start.80) | collective-permute-done | bytes 442400 | tf_op jit(solution)/shard_map/ppermute | solution.py:476
  414.7 5.6 %collective-permute-done.49 = bf16[4,48,1152]{2,1,0:T(8,128)(2,1)S(1)} collective-permute-done((bf16[4,48,1152]{2,1,0:T(8,128)(2,1)}, bf16[4,48,1152]{2,1,0:T(8,128)(2,1)S(1)}, u32[]{:S(2)}, u32[]{:S(2)}) %collective-permute-start.49) | collective-permute-done | bytes 442400 | tf_op jit(solution)/shard_map/ppermute | solution.py:476
  428.5 7.8 %collective-permute-done.60 = bf16[48,1536]{1,0:T(8,128)(2,1)S(1)} collective-permute-done((bf16[48,1536]{1,0:T(8,128)(2,1)S(1)}, bf16[48,1536]{1,0:T(8,128)(2,1)S(1)}, u32[]{:S(2)}, u32[]{:S(2)}) %collective-permute-start.60) | collective-permute-done | bytes 147488 | tf_op jit(solution)/shard_map/ppermute | solution.py:488
  442.0 5.2 %collective-permute-done.66 = bf16[144,1536]{1,0:T(8,128)(2,1)S(1)} collective-permute-done((bf16[144,1536]{1,0:T(8,128)(2,1)S(1)}, bf16[144,1536]{1,0:T(8,128)(2,1)S(1)}, u32[]{:S(2)}, u32[]{:S(2)}) %collective-permute-start.66) | collective-permute-done | bytes 442400 | tf_op jit(solution)/shard_map/ppermute | solution.py:476
  450.9 2.6 collective-permute-start.53
  459.2 2.4 collective-permute-done.68
  468.4 3.0 fusion.39
  473.6 3.7 finish.2
  477.9 3.7 finish.3
  (610 shorter events, 225.1 us)
Async XLA Ops:
  7.3 57.9 %all-gather.5.cloned.1.call-start = ((), (), s32[]{:S(2)}) async-start(), calls=%async_computation.6 | async-start | bytes 1843200 | tf_op jit(solution)/shard_map/all_gather | solution.py:1310
  7.3 12.0 %collective-permute-start.6 = (s32[2]{0:T(128)}, s32[2]{0:T(128)S(1)}, u32[]{:S(2)}, u32[]{:S(2)}) collective-permute-start(s32[2]{0:T(128)} %param.19), channel_id=1, source_target_pairs={{0,24},{8,0},{16,8},{24,16},{1,25},{9,1},{17,9},{25,17},{2,26},{10... | collective-permute-start | bytes 32 | tf_op jit(solution)/shard_map/ppermute | solution.py:488
  19.4 11.1 %collective-permute-start = (s32[128]{0:T(128)S(1)}, s32[128]{0:T(128)S(1)}, u32[]{:S(2)}, u32[]{:S(2)}) collective-permute-start(s32[128]{0:T(128)S(1)} %get-tuple-element.282), channel_id=1, source_target_pairs={{0,4},{4,0},{1,5},{5,1},{2,6},{6,2},{3,7},{7,3},{8,12},{12,8},{9,1... | collective-permute-start | bytes 1544 | tf_op jit(solution)/shard_map/ppermute | solution.py:476
  20.9 23.2 %collective-permute-start.3 = (bf16[128,768]{1,0:T(8,128)(2,1)S(1)}, bf16[128,768]{1,0:T(8,128)(2,1)S(1)}, u32[]{:S(2)}, u32[]{:S(2)}) collective-permute-start(bf16[128,768]{1,0:T(8,128)(2,1)S(1)} %get-tuple-element.228), channel_id=1, source_target_pairs={{0,4},{4,0},{1,5},{5,1},{2,6},{6,2},{3,7},{7,3},{8,12},{12,8},{9,1... | collective-permute-start | bytes 589832 | tf_op jit(solution)/shard_map/ppermute | solution.py:476
  30.4 104.0 %all-gather.7.cloned.1.call-start = ((), (), s32[]{:S(2)}) async-start(), calls=%async_computation.7 | async-start | bytes 2764800 | tf_op jit(solution)/shard_map/all_gather | solution.py:1310
  43.6 352.1 %reduce-scatter.6.cloned.1.call-start = ((), (), s32[]{:S(2)}) async-start(), calls=%async_computation.4 | async-start | bytes 737280 | tf_op jit(solution)/shard_map/reduce_scatter | solution.py:1447
  68.6 25.8 %collective-permute-start.20 = (bf16[3,96,1920]{2,1,0:T(8,128)(2,1)}, bf16[3,96,1920]{2,1,0:T(8,128)(2,1)}, u32[]{:S(2)}, u32[]{:S(2)}) collective-permute-start(bf16[3,96,1920]{2,1,0:T(8,128)(2,1)} %others.2.refs_4_), channel_id=1, source_target_pairs={{0,4},{4,0},{1,5},{5,1},{2,6},{6,2},{3,7},{7,3},{8,12},{12,8},{9,1... | collective-permute-start | bytes 3317768 | tf_op jit(solution)/shard_map/ppermute | solution.py:476
  107.4 11.4 %collective-permute-start.22 = (bf16[256,768]{1,0:T(8,128)(2,1)}, bf16[256,768]{1,0:T(8,128)(2,1)S(1)}, u32[]{:S(2)}, u32[]{:S(2)}) collective-permute-start(bf16[256,768]{1,0:T(8,128)(2,1)} %get-tuple-element.100.refs_0_), channel_id=1, source_target_pairs={{0,2},{2,0},{1,3},{3,1},{4,6},{6,4},{5,7},{7,5},{8,10},{10,8},{9,1... | collective-permute-start | bytes 1179656 | tf_op jit(solution)/shard_map/ppermute | solution.py:484
  147.7 26.8 %collective-permute-start.31 = (bf16[3,96,1920]{2,1,0:T(8,128)(2,1)}, bf16[3,96,1920]{2,1,0:T(8,128)(2,1)}, u32[]{:S(2)}, u32[]{:S(2)}) collective-permute-start(bf16[3,96,1920]{2,1,0:T(8,128)(2,1)} %get-tuple-element.111.refs_4_), channel_id=1, source_target_pairs={{0,4},{4,0},{1,5},{5,1},{2,6},{6,2},{3,7},{7,3},{8,12},{12,8},{9,1... | collective-permute-start | bytes 3317768 | tf_op jit(solution)/shard_map/ppermute | solution.py:476
  170.5 18.7 %collective-permute-start.30 = (bf16[3,96,1920]{2,1,0:T(8,128)(2,1)}, bf16[3,96,1920]{2,1,0:T(8,128)(2,1)}, u32[]{:S(2)}, u32[]{:S(2)}) collective-permute-start(bf16[3,96,1920]{2,1,0:T(8,128)(2,1)} %get-tuple-element.111.refs_4_), channel_id=1, source_target_pairs={{0,1},{1,0},{2,3},{3,2},{4,5},{5,4},{6,7},{7,6},{8,9},{9,8},{10,11... | collective-permute-start | bytes 3317768 | tf_op jit(solution)/shard_map/ppermute | solution.py:480
  175.4 13.7 %collective-permute-start.32 = (bf16[3,96,1920]{2,1,0:T(8,128)(2,1)}, bf16[3,96,1920]{2,1,0:T(8,128)(2,1)}, u32[]{:S(2)}, u32[]{:S(2)}) collective-permute-start(bf16[3,96,1920]{2,1,0:T(8,128)(2,1)} %hold.7.refs_6_), channel_id=1, source_target_pairs={{0,1},{1,0},{2,3},{3,2},{4,5},{5,4},{6,7},{7,6},{8,9},{9,8},{10,11... | collective-permute-start | bytes 3317768 | tf_op jit(solution)/shard_map/ppermute | solution.py:480
  187.6 12.1 %collective-permute-start.35 = (bf16[256,768]{1,0:T(8,128)(2,1)S(1)}, bf16[256,768]{1,0:T(8,128)(2,1)S(1)}, u32[]{:S(2)}, u32[]{:S(2)}) collective-permute-start(bf16[256,768]{1,0:T(8,128)(2,1)S(1)} %get-tuple-element.117.refs_0_.refs_1_), channel_id=1, source_target_pairs={{0,2},{2,0},{1,3},{3,1},{4,6},{6,4},{5,7},{7,5},{8,10},{10,8},{9,1... | collective-permute-start | bytes 1179656 | tf_op jit(solution)/shard_map/ppermute | solution.py:484
  194.8 12.0 %collective-permute-start.33 = (bf16[256,768]{1,0:T(8,128)(2,1)S(1)}, bf16[256,768]{1,0:T(8,128)(2,1)S(1)}, u32[]{:S(2)}, u32[]{:S(2)}) collective-permute-start(bf16[256,768]{1,0:T(8,128)(2,1)S(1)} %get-tuple-element.114.refs_0_), channel_id=1, source_target_pairs={{0,2},{2,0},{1,3},{3,1},{4,6},{6,4},{5,7},{7,5},{8,10},{10,8},{9,1... | collective-permute-start | bytes 1179656 | tf_op jit(solution)/shard_map/ppermute | solution.py:484
  213.9 23.2 %collective-permute-start.36 = (bf16[256,768]{1,0:T(8,128)(2,1)S(1)}, bf16[256,768]{1,0:T(8,128)(2,1)S(1)}, u32[]{:S(2)}, u32[]{:S(2)}) collective-permute-start(bf16[256,768]{1,0:T(8,128)(2,1)S(1)} %get-tuple-element.119), channel_id=1, source_target_pairs={{0,2},{2,0},{1,3},{3,1},{4,6},{6,4},{5,7},{7,5},{8,10},{10,8},{9,1... | collective-permute-start | bytes 1179656 | tf_op jit(solution)/shard_map/ppermute | solution.py:484
  227.0 34.7 %collective-permute-start.78 = (bf16[4,2,96,768]{3,2,0,1:T(8,128)(2,1)}, bf16[4,2,96,768]{3,2,0,1:T(8,128)(2,1)}, u32[]{:S(2)}, u32[]{:S(2)}) collective-permute-start(bf16[4,2,96,768]{3,2,0,1:T(8,128)(2,1)} %bitcast.256), channel_id=1, source_target_pairs={{0,1},{1,0},{2,3},{3,2},{4,5},{5,4},{6,7},{7,6},{8,9},{9,8},{10,11... | collective-permute-start | bytes 3538952 | tf_op jit(solution)/shard_map/ppermute | solution.py:480
  230.7 55.7 %collective-permute-start.76 = (bf16[4,2,48,1536]{3,2,0,1:T(8,128)(2,1)}, bf16[4,2,48,1536]{3,2,0,1:T(8,128)(2,1)}, u32[]{:S(2)}, u32[]{:S(2)}) collective-permute-start(bf16[4,2,48,1536]{3,2,0,1:T(8,128)(2,1)} %bitcast.257), channel_id=1, source_target_pairs={{0,1},{1,0},{2,3},{3,2},{4,5},{5,4},{6,7},{7,6},{8,9},{9,8},{10,11... | collective-permute-start | bytes 3538952 | tf_op jit(solution)/shard_map/ppermute | solution.py:480
  237.1 22.7 %collective-permute-start.73 = (bf16[4,2,48,768]{3,2,0,1:T(8,128)(2,1)}, bf16[4,2,48,768]{3,2,0,1:T(8,128)(2,1)}, u32[]{:S(2)}, u32[]{:S(2)}) collective-permute-start(bf16[4,2,48,768]{3,2,0,1:T(8,128)(2,1)} %bitcast.262), channel_id=1, source_target_pairs={{0,1},{1,0},{2,3},{3,2},{4,5},{5,4},{6,7},{7,6},{8,9},{9,8},{10,11... | collective-permute-start | bytes 1769480 | tf_op jit(solution)/shard_map/ppermute | solution.py:480
  238.1 211.0 %collective-permute-start.37 = (bf16[128,768]{1,0:T(8,128)(2,1)}, bf16[128,768]{1,0:T(8,128)(2,1)}, u32[]{:S(2)}, u32[]{:S(2)}) collective-permute-start(bf16[128,768]{1,0:T(8,128)(2,1)} %get-tuple-element.222), channel_id=1, source_target_pairs={{0,4},{4,0},{1,5},{5,1},{2,6},{6,2},{3,7},{7,3},{8,12},{12,8},{9,1... | collective-permute-start | bytes 589832 | tf_op jit(solution)/shard_map/ppermute | solution.py:476
  261.1 28.5 %collective-permute-start.74 = (bf16[4,48,768]{2,1,0:T(8,128)(2,1)S(1)}, bf16[4,48,768]{2,1,0:T(8,128)(2,1)S(1)}, u32[]{:S(2)}, u32[]{:S(2)}) collective-permute-start(bf16[4,48,768]{2,1,0:T(8,128)(2,1)S(1)} %dynamic-slice_bitcast_fusion.6), channel_id=1, source_target_pairs={{0,4},{4,0},{1,5},{5,1},{2,6},{6,2},{3,7},{7,3},{8,12},{12,8},{9,1... | collective-permute-start | bytes 884744 | tf_op jit(solution)/shard_map/ppermute | solution.py:476
  264.4 71.8 %collective-permute-start.79 = (bf16[4,96,768]{2,1,0:T(8,128)(2,1)}, bf16[4,96,768]{2,1,0:T(8,128)(2,1)}, u32[]{:S(2)}, u32[]{:S(2)}) collective-permute-start(bf16[4,96,768]{2,1,0:T(8,128)(2,1)} %dynamic-slice_bitcast_fusion), channel_id=1, source_target_pairs={{0,4},{4,0},{1,5},{5,1},{2,6},{6,2},{3,7},{7,3},{8,12},{12,8},{9,1... | collective-permute-start | bytes 1769480 | tf_op jit(solution)/shard_map/ppermute | solution.py:476
  274.6 11.0 %collective-permute-start.41 = (bf16[256,768]{1,0:T(8,128)(2,1)S(1)}, bf16[256,768]{1,0:T(8,128)(2,1)S(1)}, u32[]{:S(2)}, u32[]{:S(2)}) collective-permute-start(bf16[256,768]{1,0:T(8,128)(2,1)S(1)} %get-tuple-element.134), channel_id=1, source_target_pairs={{0,2},{2,0},{1,3},{3,1},{4,6},{6,4},{5,7},{7,5},{8,10},{10,8},{9,1... | collective-permute-start | bytes 1179656 | tf_op jit(solution)/shard_map/ppermute | solution.py:484
  285.5 20.5 %collective-permute-start.71 = (bf16[4,2,48,1152]{3,2,0,1:T(8,128)(2,1)S(1)}, bf16[4,2,48,1152]{3,2,0,1:T(8,128)(2,1)S(1)}, u32[]{:S(2)}, u32[]{:S(2)}) collective-permute-start(bf16[4,2,48,1152]{3,2,0,1:T(8,128)(2,1)S(1)} %bitcast.313), channel_id=1, source_target_pairs={{0,1},{1,0},{2,3},{3,2},{4,5},{5,4},{6,7},{7,6},{8,9},{9,8},{10,11... | collective-permute-start | bytes 2654216 | tf_op jit(solution)/shard_map/ppermute | solution.py:480
  286.4 12.0 %collective-permute-start.42 = (bf16[256,768]{1,0:T(8,128)(2,1)S(1)}, bf16[256,768]{1,0:T(8,128)(2,1)S(1)}, u32[]{:S(2)}, u32[]{:S(2)}) collective-permute-start(bf16[256,768]{1,0:T(8,128)(2,1)S(1)} %get-tuple-element.137.refs_0_), channel_id=1, source_target_pairs={{0,2},{2,0},{1,3},{3,1},{4,6},{6,4},{5,7},{7,5},{8,10},{10,8},{9,1... | collective-permute-start | bytes 1179656 | tf_op jit(solution)/shard_map/ppermute | solution.py:484
  289.8 28.2 %collective-permute-start.75 = (bf16[4,48,384]{2,1,0:T(8,128)(2,1)S(1)}, bf16[4,48,384]{2,1,0:T(8,128)(2,1)S(1)}, u32[]{:S(2)}, u32[]{:S(2)}) collective-permute-start(bf16[4,48,384]{2,1,0:T(8,128)(2,1)S(1)} %constant_dynamic-slice_fusion.4), channel_id=1, source_target_pairs={{0,2},{2,0},{1,3},{3,1},{4,6},{6,4},{5,7},{7,5},{8,10},{10,8},{9,1... | collective-permute-start | bytes 442376 | tf_op jit(solution)/shard_map/ppermute | solution.py:484
  306.3 26.1 %collective-permute-start.72 = (bf16[4,48,1152]{2,1,0:T(8,128)(2,1)S(1)}, bf16[4,48,1152]{2,1,0:T(8,128)(2,1)S(1)}, u32[]{:S(2)}, u32[]{:S(2)}) collective-permute-start(bf16[4,48,1152]{2,1,0:T(8,128)(2,1)S(1)} %dynamic-slice_bitcast_fusion.4), channel_id=1, source_target_pairs={{0,4},{4,0},{1,5},{5,1},{2,6},{6,2},{3,7},{7,3},{8,12},{12,8},{9,1... | collective-permute-start | bytes 1327112 | tf_op jit(solution)/shard_map/ppermute | solution.py:476
  314.9 22.9 %collective-permute-start.77 = (bf16[4,48,1536]{2,1,0:T(8,128)(2,1)}, bf16[4,48,1536]{2,1,0:T(8,128)(2,1)}, u32[]{:S(2)}, u32[]{:S(2)}) collective-permute-start(bf16[4,48,1536]{2,1,0:T(8,128)(2,1)} %dynamic-slice_bitcast_fusion.1), channel_id=1, source_target_pairs={{0,4},{4,0},{1,5},{5,1},{2,6},{6,2},{3,7},{7,3},{8,12},{12,8},{9,1... | collective-permute-start | bytes 1769480 | tf_op jit(solution)/shard_map/ppermute | solution.py:476
  336.2 59.4 %reduce-scatter.8.cloned.1.call-start = ((), (), s32[]{:S(2)}) async-start(), calls=%async_computation.5 | async-start | bytes 1474560 | tf_op jit(solution)/shard_map/reduce_scatter | solution.py:1447
  340.3 96.1 %reduce-scatter.4.cloned.1.call-start = ((), (), s32[]{:S(2)}) async-start(), calls=%async_computation.3 | async-start | bytes 1474560 | tf_op jit(solution)/shard_map/reduce_scatter | solution.py:1447
  346.1 12.4 %collective-permute-start.64 = (bf16[4,2,96,768]{3,2,0,1:T(8,128)(2,1)}, bf16[4,2,96,768]{3,2,0,1:T(8,128)(2,1)}, u32[]{:S(2)}, u32[]{:S(2)}) collective-permute-start(bf16[4,2,96,768]{3,2,0,1:T(8,128)(2,1)} %bitcast.258), channel_id=1, source_target_pairs={{0,1},{1,0},{2,3},{3,2},{4,5},{5,4},{6,7},{7,6},{8,9},{9,8},{10,11... | collective-permute-start | bytes 3538952 | tf_op jit(solution)/shard_map/ppermute | solution.py:480
  350.8 10.9 %collective-permute-start.62 = (bf16[4,2,48,1536]{3,2,0,1:T(8,128)(2,1)}, bf16[4,2,48,1536]{3,2,0,1:T(8,128)(2,1)}, u32[]{:S(2)}, u32[]{:S(2)}) collective-permute-start(bf16[4,2,48,1536]{3,2,0,1:T(8,128)(2,1)} %bitcast.259), channel_id=1, source_target_pairs={{0,1},{1,0},{2,3},{3,2},{4,5},{5,4},{6,7},{7,6},{8,9},{9,8},{10,11... | collective-permute-start | bytes 3538952 | tf_op jit(solution)/shard_map/ppermute | solution.py:480
  353.8 14.7 %collective-permute-start.45 = (bf16[512,768]{1,0:T(8,128)(2,1)}, bf16[512,768]{1,0:T(8,128)(2,1)S(1)}, u32[]{:S(2)}, u32[]{:S(2)}) collective-permute-start(bf16[512,768]{1,0:T(8,128)(2,1)} %copy-done.81), channel_id=1, source_target_pairs={{0,1},{1,0},{2,3},{3,2},{4,5},{5,4},{6,7},{7,6},{8,9},{9,8},{10,11... | collective-permute-start | bytes 2359304 | tf_op jit(solution)/shard_map/ppermute | solution.py:480
  361.1 27.3 %collective-permute-start.65 = (bf16[4,96,768]{2,1,0:T(8,128)(2,1)}, bf16[4,96,768]{2,1,0:T(8,128)(2,1)}, u32[]{:S(2)}, u32[]{:S(2)}) collective-permute-start(bf16[4,96,768]{2,1,0:T(8,128)(2,1)} %dynamic-slice_bitcast_fusion.2), channel_id=1, source_target_pairs={{0,4},{4,0},{1,5},{5,1},{2,6},{6,2},{3,7},{7,3},{8,12},{12,8},{9,1... | collective-permute-start | bytes 1769480 | tf_op jit(solution)/shard_map/ppermute | solution.py:476
  364.2 27.6 %collective-permute-start.63 = (bf16[4,48,1536]{2,1,0:T(8,128)(2,1)}, bf16[4,48,1536]{2,1,0:T(8,128)(2,1)}, u32[]{:S(2)}, u32[]{:S(2)}) collective-permute-start(bf16[4,48,1536]{2,1,0:T(8,128)(2,1)} %dynamic-slice_bitcast_fusion.3), channel_id=1, source_target_pairs={{0,4},{4,0},{1,5},{5,1},{2,6},{6,2},{3,7},{7,3},{8,12},{12,8},{9,1... | collective-permute-start | bytes 1769480 | tf_op jit(solution)/shard_map/ppermute | solution.py:476
  367.1 13.2 %collective-permute-start.58 = (bf16[4,48,384]{2,1,0:T(8,128)(2,1)S(1)}, bf16[4,48,384]{2,1,0:T(8,128)(2,1)S(1)}, u32[]{:S(2)}, u32[]{:S(2)}) collective-permute-start(bf16[4,48,384]{2,1,0:T(8,128)(2,1)S(1)} %constant_dynamic-slice_fusion.13), channel_id=1, source_target_pairs={{0,2},{2,0},{1,3},{3,1},{4,6},{6,4},{5,7},{7,5},{8,10},{10,8},{9,1... | collective-permute-start | bytes 442376 | tf_op jit(solution)/shard_map/ppermute | solution.py:484
  380.3 20.0 %collective-permute-start.48 = (bf16[4,2,48,1152]{3,2,0,1:T(8,128)(2,1)}, bf16[4,2,48,1152]{3,2,0,1:T(8,128)(2,1)}, u32[]{:S(2)}, u32[]{:S(2)}) collective-permute-start(bf16[4,2,48,1152]{3,2,0,1:T(8,128)(2,1)} %bitcast.261), channel_id=1, source_target_pairs={{0,1},{1,0},{2,3},{3,2},{4,5},{5,4},{6,7},{7,6},{8,9},{9,8},{10,11... | collective-permute-start | bytes 2654216 | tf_op jit(solution)/shard_map/ppermute | solution.py:480
  397.5 13.3 %collective-permute-start.80 = (bf16[144,1536]{1,0:T(8,128)(2,1)}, bf16[144,1536]{1,0:T(8,128)(2,1)S(1)}, u32[]{:S(2)}, u32[]{:S(2)}) collective-permute-start(bf16[144,1536]{1,0:T(8,128)(2,1)} %get-tuple-element.215), channel_id=1, source_target_pairs={{0,4},{4,0},{1,5},{5,1},{2,6},{6,2},{3,7},{7,3},{8,12},{12,8},{9,1... | collective-permute-start | bytes 1327112 | tf_op jit(solution)/shard_map/ppermute | solution.py:476
  398.9 13.4 %collective-permute-start.81 = (bf16[144,1536]{1,0:T(8,128)(2,1)}, bf16[144,1536]{1,0:T(8,128)(2,1)}, u32[]{:S(2)}, u32[]{:S(2)}) collective-permute-start(bf16[144,1536]{1,0:T(8,128)(2,1)} %get-tuple-element.215), channel_id=1, source_target_pairs={{0,2},{2,0},{1,3},{3,1},{4,6},{6,4},{5,7},{7,5},{8,10},{10,8},{9,1... | collective-permute-start | bytes 1327112 | tf_op jit(solution)/shard_map/ppermute | solution.py:484
  402.6 17.7 %collective-permute-start.49 = (bf16[4,48,1152]{2,1,0:T(8,128)(2,1)}, bf16[4,48,1152]{2,1,0:T(8,128)(2,1)S(1)}, u32[]{:S(2)}, u32[]{:S(2)}) collective-permute-start(bf16[4,48,1152]{2,1,0:T(8,128)(2,1)} %dynamic-slice_bitcast_fusion.5), channel_id=1, source_target_pairs={{0,4},{4,0},{1,5},{5,1},{2,6},{6,2},{3,7},{7,3},{8,12},{12,8},{9,1... | collective-permute-start | bytes 1327112 | tf_op jit(solution)/shard_map/ppermute | solution.py:476
  410.8 14.1 %collective-permute-start.83 = (bf16[80,1536]{1,0:T(8,128)(2,1)S(1)}, bf16[80,1536]{1,0:T(8,128)(2,1)S(1)}, u32[]{:S(2)}, u32[]{:S(2)}) collective-permute-start(bf16[80,1536]{1,0:T(8,128)(2,1)S(1)} %slice.270), channel_id=1, source_target_pairs={{0,2},{2,0},{1,3},{3,1},{4,6},{6,4},{5,7},{7,5},{8,10},{10,8},{9,1... | collective-permute-start | bytes 737288 | tf_op jit(solution)/shard_map/ppermute | solution.py:484
  413.2 11.5 %collective-permute-start.82 = (bf16[64,1536]{1,0:T(8,128)(2,1)S(1)}, bf16[64,1536]{1,0:T(8,128)(2,1)S(1)}, u32[]{:S(2)}, u32[]{:S(2)}) collective-permute-start(bf16[64,1536]{1,0:T(8,128)(2,1)S(1)} %slice.269), channel_id=1, source_target_pairs={{0,4},{4,0},{1,5},{5,1},{2,6},{6,2},{3,7},{7,3},{8,12},{12,8},{9,1... | collective-permute-start | bytes 589832 | tf_op jit(solution)/shard_map/ppermute | solution.py:476
  424.7 11.6 %collective-permute-start.60 = (bf16[48,1536]{1,0:T(8,128)(2,1)S(1)}, bf16[48,1536]{1,0:T(8,128)(2,1)S(1)}, u32[]{:S(2)}, u32[]{:S(2)}) collective-permute-start(bf16[48,1536]{1,0:T(8,128)(2,1)S(1)} %get-tuple-element.211), channel_id=1, source_target_pairs={{0,16},{8,24},{16,0},{24,8},{1,17},{9,25},{17,1},{25,9},{2,18},{10... | collective-permute-start | bytes 442376 | tf_op jit(solution)/shard_map/ppermute | solution.py:488
  424.9 11.4 %collective-permute-start.59 = (bf16[48,1536]{1,0:T(8,128)(2,1)S(1)}, bf16[48,1536]{1,0:T(8,128)(2,1)S(1)}, u32[]{:S(2)}, u32[]{:S(2)}) collective-permute-start(bf16[48,1536]{1,0:T(8,128)(2,1)S(1)} %get-tuple-element.210), channel_id=1, source_target_pairs={{0,8},{8,16},{16,24},{24,0},{1,9},{9,17},{17,25},{25,1},{2,10},{10... | collective-permute-start | bytes 442376 | tf_op jit(solution)/shard_map/ppermute | solution.py:488
  426.6 13.7 %collective-permute-start.51 = (f32[2,4,2496]{2,1,0:T(4,128)S(1)}, f32[2,4,2496]{2,1,0:T(4,128)S(1)}, u32[]{:S(2)}, u32[]{:S(2)}) collective-permute-start(f32[2,4,2496]{2,1,0:T(4,128)S(1)} %add.345), channel_id=1, source_target_pairs={{0,1},{1,0},{2,3},{3,2},{4,5},{5,4},{6,7},{7,6},{8,9},{9,8},{10,11... | collective-permute-start | bytes 239624 | tf_op jit(solution)/shard_map/ppermute | solution.py:480
  440.2 31.8 %collective-permute-start.84 = (bf16[4,144,1536]{2,1,0:T(8,128)(2,1)S(1)}, bf16[4,144,1536]{2,1,0:T(8,128)(2,1)S(1)}, u32[]{:S(2)}, u32[]{:S(2)}) collective-permute-start(bf16[4,144,1536]{2,1,0:T(8,128)(2,1)S(1)} %fusion.9), channel_id=1, source_target_pairs={{0,1},{1,0},{2,3},{3,2},{4,5},{5,4},{6,7},{7,6},{8,9},{9,8},{10,11... | collective-permute-start | bytes 5308424 | tf_op jit(solution)/shard_map/ppermute | solution.py:480
  440.3 13.2 %collective-permute-start.67 = (bf16[144,1536]{1,0:T(8,128)(2,1)S(1)}, bf16[144,1536]{1,0:T(8,128)(2,1)S(1)}, u32[]{:S(2)}, u32[]{:S(2)}) collective-permute-start(bf16[144,1536]{1,0:T(8,128)(2,1)S(1)} %get-tuple-element.217), channel_id=1, source_target_pairs={{0,2},{2,0},{1,3},{3,1},{4,6},{6,4},{5,7},{7,5},{8,10},{10,8},{9,1... | collective-permute-start | bytes 1327112 | tf_op jit(solution)/shard_map/ppermute | solution.py:484
  441.9 11.7 %collective-permute-start.54 = (f32[2,2496]{1,0:T(2,128)S(1)}, f32[2,2496]{1,0:T(2,128)S(1)}, u32[]{:S(2)}, u32[]{:S(2)}) collective-permute-start(f32[2,2496]{1,0:T(2,128)S(1)} %bitcast.340), channel_id=1, source_target_pairs={{0,24},{8,0},{16,8},{24,16},{1,25},{9,1},{17,9},{25,17},{2,26},{10... | collective-permute-start | bytes 59912 | tf_op jit(solution)/shard_map/ppermute | solution.py:488
  447.2 14.4 %collective-permute-start.69 = (bf16[80,1536]{1,0:T(8,128)(2,1)S(1)}, bf16[80,1536]{1,0:T(8,128)(2,1)S(1)}, u32[]{:S(2)}, u32[]{:S(2)}) collective-permute-start(bf16[80,1536]{1,0:T(8,128)(2,1)S(1)} %slice.262), channel_id=1, source_target_pairs={{0,2},{2,0},{1,3},{3,1},{4,6},{6,4},{5,7},{7,5},{8,10},{10,8},{9,1... | collective-permute-start | bytes 737288 | tf_op jit(solution)/shard_map/ppermute | solution.py:484
  461.9 15.5 %collective-permute-start.70 = (bf16[4,144,1536]{2,1,0:T(8,128)(2,1)S(1)}, bf16[4,144,1536]{2,1,0:T(8,128)(2,1)S(1)}, u32[]{:S(2)}, u32[]{:S(2)}) collective-permute-start(bf16[4,144,1536]{2,1,0:T(8,128)(2,1)S(1)} %fusion.13), channel_id=1, source_target_pairs={{0,1},{1,0},{2,3},{3,2},{4,5},{5,4},{6,7},{7,6},{8,9},{9,8},{10,11... | collective-permute-start | bytes 5308424 | tf_op jit(solution)/shard_map/ppermute | solution.py:480
  (163 other events, 1051.2 us)
Sparse Core Ops, SparseCore 0:
  30.5 34.5 all-gather.4
  67.3 46.9 all-gather.6
  336.3 21.6 reduce-scatter.5
  360.2 27.5 reduce-scatter.7
  395.7 28.7 reduce-scatter.3
